TPU v7x, 128 devices: a whole 4x4x4 slice. The times are simulated.
128 devices in a mesh: seq: 16 (over z, y_lo, core), head: 8 (over x, y_hi).
Axes of the slice: x: 4, y: 4 (y_hi: 2, y_lo: 2; y = y_hi * 2 + y_lo), z: 4, core: 2. Of those that a mesh axis runs over, the one named last changes fastest.
Arguments:
- query_in: bfloat16 [3072, 4096], P(('seq', 'head')), may hold values from -6 to 6
- key_in: bfloat16 [3072, 4096], P(('seq', 'head')), may hold values from -6 to 6
- value_in: bfloat16 [3072, 4096], P(('seq', 'head')), may hold values from -6 to 6
- grad_out: bfloat16 [3072, 4096], P(('seq', 'head')), may hold values from -6 to 6
- kernel: float32 [3, 3, 4096], P(None, None, 'head'), may hold values from 0.2 to 1
- lengths: int32 [12], replicated, may hold values from 1 to 1920, 3072 in all
Outputs:
- attended: bfloat16 [3072, 4096], P(('seq', 'head'))
- grad_query: bfloat16 [3072, 4096], P(('seq', 'head'))
- grad_key: bfloat16 [3072, 4096], P(('seq', 'head'))
- grad_value: bfloat16 [3072, 4096], P(('seq', 'head'))
Inputs may be any that keep to these rules, and one draw needn't show every extreme that they name: 12 document lengths that sum to 3072; the longest is exactly 1920.
All inputs are finite; a program needn't handle non-finite values.
Results may differ from a plain program's by a relative error of at most 0.013.
The roundings to bfloat16 on the way count: a program that leaves them out, or rounds other values in their place, can miss the bound.
Values may be sent and summed in bfloat16 or wider, within the bound.
A program may use at most 128 MiB of HBM per device.

v0:
```python
import jax
import jax.numpy as jnp
from jax import lax
from jax.sharding import PartitionSpec as P

HEAD_DIM = 128


MASKED = -1e30


def passed_along(value, axis, steps):
    count = lax.axis_size(axis)
    initial, last = (max(0, -steps), min(count, count - steps))
    return lax.ppermute(value, axis, [(source, source + steps) for source in range(initial, last)])


def segment_of(positions, doc_ends):
    return jnp.sum((positions[:, None] >= doc_ends[None, :]).astype(jnp.int32), axis=1)


def split_heads(values):
    return values.reshape(values.shape[0], -1, HEAD_DIM)


def tile_masks(query_pos, query_seg, key_pos, key_seg):
    allowed = (key_pos[None, :] <= query_pos[:, None]) & (key_seg[None, :] == query_seg[:, None])
    return allowed[None, :, :]


def tile_scores(query_rows, key_rows, allowed, scaling):
    scores = (
        jnp.einsum(
            "qhd,khd->hqk",
            split_heads(query_rows),
            split_heads(key_rows),
            preferred_element_type=jnp.float32,
        )
        * scaling
    )
    return jnp.where(allowed, scores, MASKED)


def tile_grads(query_rows, key_rows, value_rows, grad_rows, log_norm, delta_rows, allowed, scaling):
    scores = tile_scores(query_rows, key_rows, allowed, scaling)
    probabilities = jnp.where(allowed, jnp.exp(scores - log_norm.T[:, :, None]), 0.0)
    dprobs = jnp.einsum(
        "qhd,khd->hqk",
        split_heads(grad_rows),
        split_heads(value_rows),
        preferred_element_type=jnp.float32,
    )
    dscores = (probabilities * (dprobs - delta_rows.T[:, :, None])).astype(jnp.bfloat16)
    return (dscores, probabilities.astype(jnp.bfloat16))


def attend_update(
    carried, key_rows, value_rows, key_pos, key_seg, query_rows, query_pos, query_seg, scaling
):
    maxima, totals, running = carried
    allowed = tile_masks(query_pos, query_seg, key_pos, key_seg)
    scores = tile_scores(query_rows, key_rows, allowed, scaling)
    new_max = jnp.maximum(maxima, jnp.max(scores, axis=-1))
    factor = jnp.exp(maxima - new_max)
    weights = jnp.where(allowed, jnp.exp(scores - new_max[:, :, None]), 0.0)
    totals = jnp.sum(weights, axis=-1)
    values = split_heads(value_rows).astype(jnp.float32)
    running = running * factor.T[:, :, None] + jnp.einsum(
        "hqk,khd->qhd", weights, values, precision=lax.Precision.HIGHEST
    )
    return (new_max, totals, running)


def keys_gradient(
    query_rows,
    grad_rows,
    norm_rows,
    delta_rows,
    query_pos,
    query_seg,
    key_rows,
    value_rows,
    key_pos,
    key_seg,
    scaling,
):
    allowed = tile_masks(query_pos, query_seg, key_pos, key_seg)
    dscores, probs_low = tile_grads(
        query_rows, key_rows, value_rows, grad_rows, norm_rows, delta_rows, allowed, scaling
    )
    more_key = (
        jnp.einsum(
            "hqk,qhd->khd", dscores, split_heads(query_rows), preferred_element_type=jnp.float32
        )
        * scaling
    )
    more_value = jnp.einsum(
        "hqk,qhd->khd", probs_low, split_heads(grad_rows), preferred_element_type=jnp.float32
    )
    return (more_key, more_value)


def on_device(query_in, key_in, value_in, grad_out, kernel, lengths):
    query_rows, key_rows, value_rows, grad_rows = (
        lax.all_to_all(query_in, "head", split_axis=1, concat_axis=0, tiled=True),
        lax.all_to_all(key_in, "head", split_axis=1, concat_axis=0, tiled=True),
        lax.all_to_all(value_in, "head", split_axis=1, concat_axis=0, tiled=True),
        lax.all_to_all(grad_out, "head", split_axis=1, concat_axis=0, tiled=True),
    )
    block_rows = query_rows.shape[0]
    row_width = query_rows.shape[1]
    head_count = row_width // HEAD_DIM
    scaling = HEAD_DIM ** (-0.5)
    doc_ends = jnp.cumsum(lengths)
    first_row = lax.axis_index("seq") * block_rows
    positions = first_row + jnp.arange(block_rows, dtype=jnp.int32)
    segments = segment_of(positions, doc_ends)
    stacked = jnp.stack((query_rows, key_rows, value_rows))
    earlier_part = passed_along(stacked[:, block_rows - 2 :, :], "seq", 1)
    extended = jnp.concatenate((earlier_part, stacked), axis=1).astype(jnp.float32)
    wide_segments = segment_of(
        first_row - 2 + jnp.arange(block_rows + 2, dtype=jnp.int32), doc_ends
    )
    same_one = (wide_segments[1:-1] == segments)[None, :, None]
    same_two = (wide_segments[:-2] == segments)[None, :, None]
    mixture = kernel[:, 0][:, None, :] * extended[:, 2:] + kernel[:, 1][:, None, :] * jnp.where(
        same_one, extended[:, 1:-1], 0.0
    )
    mixture = mixture + kernel[:, 2][:, None, :] * jnp.where(same_two, extended[:, :-2], 0.0)
    convolved = mixture.astype(jnp.bfloat16)
    query_conv = convolved[0]
    key_conv = convolved[1]
    value_conv = convolved[2]
    initial = (
        jnp.full((head_count, block_rows), MASKED, jnp.float32),
        jnp.zeros((head_count, block_rows), jnp.float32),
        jnp.zeros((block_rows, head_count, HEAD_DIM), jnp.float32),
    )
    key_piece = lax.all_gather(key_conv, "seq", axis=0, tiled=True)
    value_piece = lax.all_gather(value_conv, "seq", axis=0, tiled=True)
    row_count = key_piece.shape[0]
    key_pos = jnp.arange(row_count, dtype=jnp.int32)
    key_seg = segment_of(key_pos, doc_ends)
    maxima, totals, running = attend_update(
        initial, key_piece, value_piece, key_pos, key_seg, query_conv, positions, segments, scaling
    )
    attended = running / totals.T[:, :, None]
    log_norm = (maxima + jnp.log(totals)).T
    delta_rows = jnp.sum(split_heads(grad_rows).astype(jnp.float32) * attended, axis=-1)
    all_norms, all_deltas = (
        lax.all_gather(log_norm, "seq", axis=0, tiled=True),
        lax.all_gather(delta_rows, "seq", axis=0, tiled=True),
    )
    key_piece = lax.all_gather(key_conv, "seq", axis=0, tiled=True)
    value_piece = lax.all_gather(value_conv, "seq", axis=0, tiled=True)
    query_piece = lax.all_gather(query_conv, "seq", axis=0, tiled=True)
    grad_piece = lax.all_gather(grad_rows, "seq", axis=0, tiled=True)
    row_count = key_piece.shape[0]
    other_pos = jnp.arange(row_count, dtype=jnp.int32)
    other_seg = segment_of(other_pos, doc_ends)
    allowed = tile_masks(positions, segments, other_pos, other_seg)
    dscores = tile_grads(
        query_conv, key_piece, value_piece, grad_rows, log_norm, delta_rows, allowed, scaling
    )[0]
    grad_query = (
        jnp.einsum(
            "hqk,khd->qhd", dscores, split_heads(key_piece), preferred_element_type=jnp.float32
        )
        * scaling
    )
    more_key, more_value = keys_gradient(
        query_piece,
        grad_piece,
        all_norms,
        all_deltas,
        other_pos,
        other_seg,
        key_conv,
        value_conv,
        positions,
        segments,
        scaling,
    )
    grad_key = more_key
    grad_value = more_value
    grad_query, grad_key, grad_value = (grad_query, grad_key, grad_value)
    conv_grads = jnp.stack(
        (
            grad_query.reshape(block_rows, row_width),
            grad_key.reshape(block_rows, row_width),
            grad_value.reshape(block_rows, row_width),
        )
    )
    following_rows = passed_along(conv_grads[:, :2, :], "seq", -1)
    following = jnp.concatenate((conv_grads, following_rows), axis=1)
    next_segments = segment_of(first_row + jnp.arange(block_rows + 2, dtype=jnp.int32), doc_ends)
    after_one = (next_segments[1:-1] == segments)[None, :, None]
    after_two = (next_segments[2:] == segments)[None, :, None]
    inputs_grad = kernel[:, 0][:, None, :] * conv_grads + kernel[:, 1][:, None, :] * jnp.where(
        after_one, following[:, 1:-1], 0.0
    )
    inputs_grad = (
        inputs_grad + kernel[:, 2][:, None, :] * jnp.where(after_two, following[:, 2:], 0.0)
    ).astype(jnp.bfloat16)
    attended_out = attended.reshape(block_rows, row_width).astype(jnp.bfloat16)
    returned = (
        lax.all_to_all(attended_out, "head", split_axis=0, concat_axis=1, tiled=True),
        lax.all_to_all(inputs_grad[0], "head", split_axis=0, concat_axis=1, tiled=True),
        lax.all_to_all(inputs_grad[1], "head", split_axis=0, concat_axis=1, tiled=True),
        lax.all_to_all(inputs_grad[2], "head", split_axis=0, concat_axis=1, tiled=True),
    )
    return (returned[0], returned[1], returned[2], returned[3])


def solution(mesh):
    placed = (
        P(("seq", "head"), None),
        P(("seq", "head"), None),
        P(("seq", "head"), None),
        P(("seq", "head"), None),
        P(None, None, "head"),
        P(),
    )
    return jax.shard_map(
        on_device,
        mesh=mesh,
        in_specs=placed,
        out_specs=(
            P(("seq", "head"), None),
            P(("seq", "head"), None),
            P(("seq", "head"), None),
            P(("seq", "head"), None),
        ),
        check_vma=False,
    )
```

profile of v0, /device:TPU:1, one launch (start us, length us, event | category | flops | bytes accessed | tf_op | source)
XLA Modules:
  0.0 285.8 jit_solution(13857463201494935527)
XLA Ops:
  8.2 14.5 %all_to_all.140 = bf16[24,8,512]{2,0,1:T(8,128)(2,1)} all-to-all(bf16[24,8,512]{2,0,1:T(8,128)(2,1)S(1)} %bitcast.139), channel_id=1, replica_groups=mesh['seq'=16,'head'=8] {'head'}, dimensions={1} | all-to-all | bytes 393216 | tf_op jit(solution)/shard_map/all_to_all | solution.py:108
  24.3 3.4 %all-to-all-start.2 = ((bf16[24,8,512]{2,0,1:T(8,128)(2,1)}), bf16[24,8,512]{2,0,1:T(8,128)(2,1)S(1)}, u32[]{:S(2)}, u32[]{:S(2)}) async-start(bf16[24,8,512]{2,0,1:T(8,128)(2,1)} %bitcast.113), calls=%async_computation.2 | async-start | bytes 393216 | tf_op jit(solution)/shard_map/all_to_all | solution.py:107
  34.7 3.8 %all-to-all-start.1 = ((bf16[24,8,512]{2,0,1:T(8,128)(2,1)}), bf16[24,8,512]{2,0,1:T(8,128)(2,1)S(1)}, u32[]{:S(2)}, u32[]{:S(2)}) async-start(bf16[24,8,512]{2,0,1:T(8,128)(2,1)} %bitcast.114), calls=%async_computation.1 | async-start | bytes 393216 | tf_op jit(solution)/shard_map/all_to_all | solution.py:106
  39.4 6.3 %all-to-all-done.1 = bf16[24,8,512]{2,0,1:T(8,128)(2,1)S(1)} async-done(((bf16[24,8,512]{2,0,1:T(8,128)(2,1)}), bf16[24,8,512]{2,0,1:T(8,128)(2,1)S(1)}, u32[]{:S(2)}, u32[]{:S(2)}) %all-to-all-start.1) | async-done | bytes 196640 | tf_op jit(solution)/shard_map/all_to_all | solution.py:106
  45.7 3.4 %all-to-all-start = ((bf16[24,8,512]{2,0,1:T(8,128)(2,1)}), bf16[24,8,512]{2,0,1:T(8,128)(2,1)S(1)}, u32[]{:S(2)}, u32[]{:S(2)}) async-start(bf16[24,8,512]{2,0,1:T(8,128)(2,1)} %bitcast.115), calls=%async_computation | async-start | bytes 393216 | tf_op jit(solution)/shard_map/all_to_all | solution.py:105
  49.1 7.0 %all-to-all-done = bf16[24,8,512]{2,0,1:T(8,128)(2,1)S(1)} async-done(((bf16[24,8,512]{2,0,1:T(8,128)(2,1)}), bf16[24,8,512]{2,0,1:T(8,128)(2,1)S(1)}, u32[]{:S(2)}, u32[]{:S(2)}) %all-to-all-start) | async-done | bytes 196640 | tf_op jit(solution)/shard_map/all_to_all | solution.py:105
  56.1 7.1 %collective-permute-start = (bf16[3,2,512]{2,1,0:T(2,128)(2,1)S(1)}, bf16[3,2,512]{2,1,0:T(2,128)(2,1)S(1)}, u32[]{:S(2)}, u32[]{:S(2)}) collective-permute-start(bf16[3,2,512]{2,1,0:T(2,128)(2,1)S(1)} %pad_maximum_fusion.1), channel_id=1, source_target_pairs={{0,8},{8,16},{16,24},{24,32},{32,40},{40,48},{48,56},{56,64},{64,7... | collective-permute-start | bytes 18440 | tf_op jit(solution)/shard_map/ppermute | solution.py:15
  73.9 4.7 %copy.137 = bf16[3072,512]{0,1:T(8,128)(2,1)} copy(bf16[3072,512]{1,0:T(8,128)(2,1)} %all-gather.10.cloned.1.call-done) | data formatting | bytes 6291456 | tf_op jit(solution)/shard_map/all_gather | solution.py:157
  78.7 24.1 %all-gather.12.cloned.1.call-done = bf16[1,3072,512]{2,1,0:T(8,128)(2,1)} async-done(((bf16[1,192,512]{2,1,0:T(8,128)(2,1)}), bf16[1,3072,512]{2,1,0:T(8,128)(2,1)}) %all-gather.12.cloned.1.call-update) | async-done | bytes 3145744 | tf_op jit(solution)/shard_map/all_gather | solution.py:139
  106.0 35.1 %all-gather.14.cloned.1.call-done = bf16[1,3072,512]{2,1,0:T(8,128)(2,1)} async-done(((bf16[1,192,512]{2,1,0:T(8,128)(2,1)}), bf16[1,3072,512]{2,1,0:T(8,128)(2,1)}) %all-gather.14.cloned.1.call-update) | async-done | bytes 3145744 | tf_op jit(solution)/shard_map/all_gather | solution.py:140
  141.1 4.6 %copy.123 = bf16[1,3072,512]{1,2,0:T(8,128)(2,1)} copy(bf16[1,3072,512]{2,1,0:T(8,128)(2,1)} %all-gather.14.cloned.1.call-done) | data formatting | bytes 6291456 | tf_op jit(solution)/shard_map/all_gather | solution.py:140
  145.7 3.4 %fusion.5 = (f32[4,192]{1,0:T(4,128)S(1)}, f32[4,192,3072]{2,1,0:T(8,128)S(1)}) fusion(pred[192,3072]{1,0:T(8,128)(4,1)} %fusion.14, bf16[3072,4,128]{0,2,1:T(8,128)(2,1)S(1)} %bitcast.117, bf16[192,4,128]{2,1,0:T(4,128)(2,1)S(1)} %reshape_squeeze.10), kind=kOutput, calls=%fused_computation.10 | convolution fusion | flops 611056896 | bytes 13372416 | tf_op jit(solution)/shard_map/qhd,khd->hqk/dot_general | solution.py:33
  149.2 3.4 %fusion.2 = f32[4,192]{1,0:T(4,128)S(1)} fusion(f32[4,192,3072]{2,1,0:T(8,128)S(1)} %get-tuple-element.26, f32[4,192]{1,0:T(4,128)S(1)} %broadcast_maximum_fusion, pred[192,3072]{1,0:T(8,128)(4,1)S(1)} %copy-done.1), kind=kLoop, calls=%fused_computation.7 | loop fusion | flops 11795712 | bytes 10033152 | tf_op jit(solution)/shard_map/reduce_sum | solution.py:66
  153.9 7.9 %multiply_reduce_fusion = (f32[192,4]{0,1:T(4,128)}, bf16[192,4,128]{2,0,1:T(8,128)(2,1)}) fusion(bf16[192,4,128]{2,1,0:T(4,128)(2,1)S(1)} %copy-done.9, f32[192,4]{0,1:T(4,128)S(1)} %bitcast.153, bf16[3072,4,128]{0,2,1:T(8,128)(2,1)S(1)} %bitcast.124, f32[4,192,3072]{2,1,0:T(8,128)S(1)} %get-tuple-element.26, f32[4,192]{1,0:T(4,128)S(1)} %broadcast_maximum_fusion, ...), kind=kOutput, calls=%fused_computation.52 | convolution fusion | flops 3633904896 | bytes 13578240 | tf_op jit(solution)/shard_map/hqk,khd->qhd/dot_general | solution.py:68
  161.7 10.3 %fusion.26 = f32[192,4,128]{2,0,1:T(8,128)} fusion(bf16[3072,4,128]{0,2,1:T(8,128)(2,1)S(1)} %bitcast.118, f32[4,192,3072]{2,1,0:T(8,128)} %copy-done, bf16[3072,4,128]{0,2,1:T(8,128)(2,1)} %bitcast.123, f32[4,192]{1,0:T(4,128)} %bitcast.157, f32[4,192]{1,0:T(4,128)} %log_add_fusion, pred[192,3072]{1,0:T(8,128)(4,1)} %fusion.14, ...), kind=kOutput, calls=%fused_computation.32 | convolution fusion | flops 1224572928 | bytes 16914432 | tf_op jit(solution)/shard_map/hqk,khd->qhd/dot_general | solution.py:166
  173.5 18.5 %all-gather.4 = f32[16,192,4]{1,2,0:T(4,128)S(1)} all-gather(f32[1,192,4]{1,2,0:T(4,128)} %bitcast.158), channel_id=1, replica_groups=mesh['seq'=16,'head'=8] {'seq'}, dimensions={0}, use_global_device_ids=true | all-gather | bytes 52224 | tf_op jit(solution)/shard_map/all_gather | solution.py:152
  192.7 16.7 %all-gather.3 = f32[16,192,4]{1,2,0:T(4,128)S(1)} all-gather(f32[1,192,4]{1,2,0:T(4,128)} %get-tuple-element.17), channel_id=1, replica_groups=mesh['seq'=16,'head'=8] {'seq'}, dimensions={0}, use_global_device_ids=true | all-gather | bytes 52224 | tf_op jit(solution)/shard_map/all_gather | solution.py:151
  219.3 10.2 %fusion.24 = f32[192,4,128]{2,0,1:T(8,128)} fusion(bf16[3072,4,128]{0,2,1:T(8,128)(2,1)S(1)} %bitcast.120, f32[4,3072,192]{1,2,0:T(8,128)} %copy-done.2, bf16[3072,4,128]{0,2,1:T(8,128)(2,1)} %bitcast.121, f32[4,3072]{1,0:T(4,128)} %bitcast.150, f32[4,3072]{1,0:T(4,128)} %bitcast.151, pred[3072,192]{0,1:T(8,128)(4,1)} %fusion.15, ...), kind=kOutput, calls=%fused_computation.30 | convolution fusion | flops 1224572928 | bytes 17006592 | tf_op jit(solution)/shard_map/hqk,qhd->khd/dot_general | solution.py:92
  234.5 6.2 %all-to-all-start.3 = ((bf16[8,24,512]{2,1,0:T(8,128)(2,1)}), bf16[8,24,512]{2,1,0:T(8,128)(2,1)S(1)}, u32[]{:S(2)}, u32[]{:S(2)}) async-start(bf16[8,24,512]{2,1,0:T(8,128)(2,1)} %convert_element_type.48), calls=%async_computation.3 | async-start | bytes 393216 | tf_op jit(solution)/shard_map/all_to_all | solution.py:207
  242.0 6.7 %all-to-all-done.3 = bf16[8,24,512]{2,1,0:T(8,128)(2,1)S(1)} async-done(((bf16[8,24,512]{2,1,0:T(8,128)(2,1)}), bf16[8,24,512]{2,1,0:T(8,128)(2,1)S(1)}, u32[]{:S(2)}, u32[]{:S(2)}) %all-to-all-start.3) | async-done | bytes 196640 | tf_op jit(solution)/shard_map/all_to_all | solution.py:207
  248.7 10.0 %all_to_all.141 = bf16[8,24,512]{2,1,0:T(8,128)(2,1)S(1)} all-to-all(bf16[8,24,512]{2,1,0:T(8,128)(2,1)S(1)} %bitcast.134), channel_id=1, replica_groups=mesh['seq'=16,'head'=8] {'head'}, dimensions={0} | all-to-all | bytes 393216 | tf_op jit(solution)/shard_map/all_to_all | solution.py:208
  258.7 9.5 %all_to_all.142 = bf16[8,24,512]{2,1,0:T(8,128)(2,1)S(1)} all-to-all(bf16[8,24,512]{2,1,0:T(8,128)(2,1)S(1)} %bitcast.133), channel_id=1, replica_groups=mesh['seq'=16,'head'=8] {'head'}, dimensions={0} | all-to-all | bytes 393216 | tf_op jit(solution)/shard_map/all_to_all | solution.py:209
  268.2 3.4 %all-to-all-start.7 = ((bf16[8,24,512]{2,1,0:T(8,128)(2,1)}), bf16[8,24,512]{2,1,0:T(8,128)(2,1)S(1)}, u32[]{:S(2)}, u32[]{:S(2)}) async-start(bf16[8,24,512]{2,1,0:T(8,128)(2,1)} %bitcast.32), calls=%async_computation.7 | async-start | bytes 393216 | tf_op jit(solution)/shard_map/all_to_all | solution.py:210
  273.7 4.9 %all-to-all-done.7 = bf16[8,24,512]{2,1,0:T(8,128)(2,1)S(1)} async-done(((bf16[8,24,512]{2,1,0:T(8,128)(2,1)}), bf16[8,24,512]{2,1,0:T(8,128)(2,1)S(1)}, u32[]{:S(2)}, u32[]{:S(2)}) %all-to-all-start.7) | async-done | bytes 196640 | tf_op jit(solution)/shard_map/all_to_all | solution.py:210
  (97 shorter events, 46.5 us)
Async XLA Ops:
  7.2 66.8 %all-gather.10.cloned.1.call-start = ((), (), s32[]{:S(2)}) async-start(), calls=%async_computation.8 | async-start | bytes 3342336 | tf_op jit(solution)/shard_map/all_gather | solution.py:157
  24.3 10.4 %all-to-all-start.2 = ((bf16[24,8,512]{2,0,1:T(8,128)(2,1)}), bf16[24,8,512]{2,0,1:T(8,128)(2,1)S(1)}, u32[]{:S(2)}, u32[]{:S(2)}) async-start(bf16[24,8,512]{2,0,1:T(8,128)(2,1)} %bitcast.113), calls=%async_computation.2 | async-start | bytes 393216 | tf_op jit(solution)/shard_map/all_to_all | solution.py:107
  34.7 11.0 %all-to-all-start.1 = ((bf16[24,8,512]{2,0,1:T(8,128)(2,1)}), bf16[24,8,512]{2,0,1:T(8,128)(2,1)S(1)}, u32[]{:S(2)}, u32[]{:S(2)}) async-start(bf16[24,8,512]{2,0,1:T(8,128)(2,1)} %bitcast.114), calls=%async_computation.1 | async-start | bytes 393216 | tf_op jit(solution)/shard_map/all_to_all | solution.py:106
  45.7 10.5 %all-to-all-start = ((bf16[24,8,512]{2,0,1:T(8,128)(2,1)}), bf16[24,8,512]{2,0,1:T(8,128)(2,1)S(1)}, u32[]{:S(2)}, u32[]{:S(2)}) async-start(bf16[24,8,512]{2,0,1:T(8,128)(2,1)} %bitcast.115), calls=%async_computation | async-start | bytes 393216 | tf_op jit(solution)/shard_map/all_to_all | solution.py:105
  49.1 53.8 %all-gather.12.cloned.1.call-start = ((), (), s32[]{:S(2)}) async-start(), calls=%async_computation.9 | async-start | bytes 3342336 | tf_op jit(solution)/shard_map/all_gather | solution.py:139
  56.1 7.8 %collective-permute-start = (bf16[3,2,512]{2,1,0:T(2,128)(2,1)S(1)}, bf16[3,2,512]{2,1,0:T(2,128)(2,1)S(1)}, u32[]{:S(2)}, u32[]{:S(2)}) collective-permute-start(bf16[3,2,512]{2,1,0:T(2,128)(2,1)S(1)} %pad_maximum_fusion.1), channel_id=1, source_target_pairs={{0,8},{8,16},{16,24},{24,32},{32,40},{40,48},{48,56},{56,64},{64,7... | collective-permute-start | bytes 18440 | tf_op jit(solution)/shard_map/ppermute | solution.py:15
  64.2 5.4 %copy-start.6 = (bf16[24,8,512]{2,0,1:T(8,128)(2,1)S(1)}, bf16[24,8,512]{2,0,1:T(8,128)(2,1)}, u32[]{:S(2)}) copy-start(bf16[24,8,512]{2,0,1:T(8,128)(2,1)} %all_to_all.140) | copy-start | bytes 589828
  65.6 75.5 %all-gather.14.cloned.1.call-start = ((), (), s32[]{:S(2)}) async-start(), calls=%async_computation.10 | async-start | bytes 3342336 | tf_op jit(solution)/shard_map/all_gather | solution.py:140
  66.3 144.7 %all-gather.16.cloned.1.call-start = ((), (), s32[]{:S(2)}) async-start(), calls=%async_computation.11 | async-start | bytes 3342336 | tf_op jit(solution)/shard_map/all_gather | solution.py:156
  145.7 3.5 %copy-start.1 = (pred[192,3072]{1,0:T(8,128)(4,1)S(1)}, pred[192,3072]{1,0:T(8,128)(4,1)}, u32[]{:S(2)}) copy-start(pred[192,3072]{1,0:T(8,128)(4,1)} %fusion.14) | copy-start | bytes 1769476
  149.2 4.7 %copy-start = (f32[4,192,3072]{2,1,0:T(8,128)}, f32[4,192,3072]{2,1,0:T(8,128)S(1)}, u32[]{:S(2)}) copy-start(f32[4,192,3072]{2,1,0:T(8,128)S(1)} %get-tuple-element.26) | copy-start | bytes 28311556
  149.2 4.6 %copy-start.4 = (bf16[1,3072,512]{1,2,0:T(8,128)(2,1)S(1)}, bf16[1,3072,512]{1,2,0:T(8,128)(2,1)}, u32[]{:S(2)}) copy-start(bf16[1,3072,512]{1,2,0:T(8,128)(2,1)} %copy.123) | copy-start | bytes 9437188
  149.2 4.6 %copy-start.9 = (bf16[192,4,128]{2,1,0:T(4,128)(2,1)S(1)}, bf16[192,4,128]{2,1,0:T(4,128)(2,1)}, u32[]{:S(2)}) copy-start(bf16[192,4,128]{2,1,0:T(4,128)(2,1)} %reshape.220) | copy-start | bytes 589828
  214.2 2.0 copy-start.7
  214.2 2.0 copy-start.12
  215.6 3.7 %copy-start.2 = (f32[4,3072,192]{1,2,0:T(8,128)}, f32[4,3072,192]{1,2,0:T(8,128)S(1)}, u32[]{:S(2)}) copy-start(f32[4,3072,192]{1,2,0:T(8,128)S(1)} %fusion.43) | copy-start | bytes 28311556
  229.4 2.0 copy-start.5
  229.4 4.2 %copy-start.8 = (bf16[192,4,128]{2,0,1:T(8,128)(2,1)S(1)}, bf16[192,4,128]{2,0,1:T(8,128)(2,1)}, u32[]{:S(2)}) copy-start(bf16[192,4,128]{2,0,1:T(8,128)(2,1)} %get-tuple-element.13) | copy-start | bytes 589828
  229.4 11.3 %copy-start.11 = (f32[3,1,512]{2,0,1:T(4,128)S(1)}, f32[3,1,512]{2,0,1:T(4,128)}, u32[]{:S(2)}) copy-start(f32[3,1,512]{2,0,1:T(4,128)} %copy-done.10) | copy-start | bytes 18436
  229.4 11.3 %copy-start.13 = (pred[192]{0:T(512)(128)(4,1)S(1)}, pred[192]{0:T(512)(128)(4,1)}, u32[]{:S(2)}) copy-start(pred[192]{0:T(512)(128)(4,1)} %get-tuple-element.19) | copy-start | bytes 580
  229.4 11.3 %copy-start.14 = (pred[192]{0:T(512)(128)(4,1)S(1)}, pred[192]{0:T(512)(128)(4,1)}, u32[]{:S(2)}) copy-start(pred[192]{0:T(512)(128)(4,1)} %get-tuple-element.20) | copy-start | bytes 580
  231.5 9.2 %collective-permute-start.1 = (f32[3,2,512]{2,1,0:T(2,128)S(1)}, f32[3,2,512]{2,1,0:T(2,128)S(1)}, u32[]{:S(2)}, u32[]{:S(2)}) collective-permute-start(f32[3,2,512]{2,1,0:T(2,128)S(1)} %slice.89), channel_id=1, source_target_pairs={{8,0},{16,8},{24,16},{32,24},{40,32},{48,40},{56,48},{64,56},{72,6... | collective-permute-start | bytes 36872 | tf_op jit(solution)/shard_map/ppermute | solution.py:15
  234.5 14.2 %all-to-all-start.3 = ((bf16[8,24,512]{2,1,0:T(8,128)(2,1)}), bf16[8,24,512]{2,1,0:T(8,128)(2,1)S(1)}, u32[]{:S(2)}, u32[]{:S(2)}) async-start(bf16[8,24,512]{2,1,0:T(8,128)(2,1)} %convert_element_type.48), calls=%async_computation.3 | async-start | bytes 393216 | tf_op jit(solution)/shard_map/all_to_all | solution.py:207
  268.2 10.4 %all-to-all-start.7 = ((bf16[8,24,512]{2,1,0:T(8,128)(2,1)}), bf16[8,24,512]{2,1,0:T(8,128)(2,1)S(1)}, u32[]{:S(2)}, u32[]{:S(2)}) async-start(bf16[8,24,512]{2,1,0:T(8,128)(2,1)} %bitcast.32), calls=%async_computation.7 | async-start | bytes 393216 | tf_op jit(solution)/shard_map/all_to_all | solution.py:210
  (2 other events, 3.5 us)
Sparse Core Ops, SparseCore 0:
  22.8 36.9 all-gather.9
  65.7 37.0 all-gather.11
  105.1 35.9 all-gather.13
  143.2 35.9 all-gather.15
where the time goes:
time: 291 us; the launch traced here: 286 us
  waiting for transfers between devices  88.1 us (30%)
  blocking collectives  69.2 us (24%)
  local copies, waits for them, and re-layouts  38.4 us (13%)
  matrix products  36.1 us (12%)
  starting transfers between devices  29.6 us (10%)
  between operations  14.1 us (5%)
  other arithmetic  10.4 us (4%)
    all_gather x1, waiting for transfers between devices, on_device(): value_piece = lax.all_gather(value_conv, 'seq', axis=0, tiled=True)  35.1 us
    all_gather x1, waiting for transfers between devices, on_device(): key_piece = lax.all_gather(key_conv, 'seq', axis=0, tiled=True)  24.1 us
    all_gather x1, blocking collectives, on_device(): lax.all_gather(delta_rows, 'seq', axis=0, tiled=True)  18.5 us
    all_gather x1, blocking collectives, on_device(): lax.all_gather(log_norm, 'seq', axis=0, tiled=True)  16.7 us
    all_to_all x1, blocking collectives, on_device(): lax.all_to_all(grad_out, 'head', split_axis=1, concat_axis=0, tiled=True)  14.5 us
    dot_general x1, matrix products, on_device(): jnp.einsum('hqk,khd->qhd', dscores, split_heads(key_piece), preferred_ele...  10.3 us
    dot_general x1, matrix products, keys_gradient(): jnp.einsum('hqk,qhd->khd', dscores, split_heads(query_rows), preferred_el...  10.2 us
    all_to_all x1, blocking collectives, on_device(): lax.all_to_all(inputs_grad[0], 'head', split_axis=0, concat_axis=1, tiled...  10 us
  transfers between devices with their start and end apart: 11, of which 8 were waited for; matrix products, arithmetic and copies ran while one was open for 22% of the time, Pallas kernels for 0%

commit v1 on v0

v1 whole, which is shorter than its diff:
```python
import functools

import jax
import jax.numpy as jnp
from jax import lax
from jax.experimental import pallas as pl
from jax.experimental.pallas import tpu as pltpu
from jax.sharding import Mesh
from jax.sharding import PartitionSpec as P

NAMES = ("z", "yl", "core", "x", "yh")
SIZES = (4, 2, 2, 4, 2)
D = 128
T = 3072
HEADS = 32
PIECE = 24
BLOCK = 384
PER_BLOCK = BLOCK // PIECE
OWN = 64
DOCS = 12
BQ = BLOCK
BK = 768
MASKED = -1.0e30
SCALE = D**-0.5
LOG2E = 1.4426950408889634
NT = (((1,), (1,)), ((), ()))
F32, BF16 = jnp.float32, jnp.bfloat16
MESH = pl.DeviceIdType.MESH


def dot(a, b):
    return jnp.dot(a, b, preferred_element_type=F32)


class Place:
    def __init__(self):
        self.z, self.yl, self.core, self.x, self.yh = (lax.axis_index(n) for n in NAMES)
        self.owner = lax.rem(self.x + self.z, 2) == self.yl
        self.takes = lax.rem(self.z + self.yl, 2)
        self.slot = self.z * PER_BLOCK + self.core * 8 + self.x * 2 + self.yh
        self.home = self.owner & (self.takes == self.core)

    def head_at(self, i):
        k = lax.rem(i + self.x * 8 + self.yh * 4 + self.z, HEADS)
        hx, hyh, hz = k // 8, lax.rem(k // 4, 2), lax.rem(k, 4)
        return k, dict(z=hz, yl=lax.rem(hx + hz, 2), core=self.takes, x=hx, yh=hyh)

    def token_at(self, i):
        s = lax.rem(i + self.slot, OWN)
        tz, tc, tx, tyh = s // 16, lax.rem(s // 8, 2), lax.rem(s // 2, 4), lax.rem(s, 2)
        return s, dict(z=tz, yl=lax.rem(tz + self.core, 2), core=tc, x=tx, yh=tyh)

    def sibling(self):
        return dict(z=self.z, yl=self.yl, core=1 - self.core, x=self.x, yh=self.yh)


def signal(sem, device):
    pl.semaphore_signal(sem, 1, device_id=device, device_id_type=MESH)


def remote(src, dst, send, recv, device):
    return pltpu.make_async_remote_copy(src, dst, send, recv, device_id=device, device_id_type=MESH)


def drain(ref, sem):
    pltpu.make_async_copy(ref, ref, sem).wait()


def columns(head):
    return pl.ds(pl.multiple_of(head * D, D), D)


def collect_kernel(q_ref, k_ref, v_ref, g_ref, xkv, xq, xg, xh, ssem, rsem, lsem, psem, tsem):
    me = Place()
    barrier = pltpu.get_barrier_semaphore()

    @pl.when(me.owner)
    def _():
        @pl.when(jnp.logical_not(me.home))
        def _():
            signal(barrier, me.sibling())
            _, device = me.token_at(0)
            signal(barrier, device)

        def greet(i, _):
            signal(barrier, me.token_at(i)[1])
            return 0

        lax.fori_loop(1, OWN, greet, 0)

    pl.semaphore_wait(barrier, HEADS)

    def targets(n):
        return (
            (k_ref, xkv.at[me.takes, me.slot, 0], rsem.at[0]),
            (v_ref, xkv.at[me.takes, me.slot, 1], rsem.at[0]),
            (q_ref, xq.at[me.slot], rsem.at[1]),
            (g_ref, xg.at[me.slot], rsem.at[2]),
        )[n]

    for group in ((0, 1), (2, 3)):
        def send(i, _, group=group):
            head, device = me.head_at(i)
            for n in group:
                src, dst, sem = targets(n)
                remote(src.at[:, columns(head)], dst, ssem.at[n], sem, device).start()
            return 0

        @pl.when(me.home)
        def _():
            head, _ = me.head_at(0)
            for n in group:
                src, dst, _ = targets(n)
                pltpu.make_async_copy(src.at[:, columns(head)], dst, lsem.at[n]).start()

        @pl.when(jnp.logical_not(me.home))
        def _():
            send(0, 0)

        lax.fori_loop(1, HEADS, send, 0)

    def swap():
        return remote(xkv.at[me.core], xkv.at[me.core], psem.at[0], tsem.at[0], me.sibling())

    def halo(z):
        return remote(xq.at[z * PER_BLOCK + PER_BLOCK - 1], xh.at[z], psem.at[1 + z], tsem.at[1 + z], me.sibling())

    @pl.when(me.owner)
    def _():
        @pl.when(me.home)
        def _():
            head, _ = me.head_at(0)
            for n in range(4):
                src, dst, _ = targets(n)
                pltpu.make_async_copy(src.at[:, columns(head)], dst, lsem.at[n]).wait()
            drain(xkv.at[0, pl.ds(0, OWN - 1)], rsem.at[0])

        @pl.when(jnp.logical_not(me.home))
        def _():
            drain(xkv.at[0, pl.ds(0, OWN)], rsem.at[0])

        swap().start()

        @pl.when(me.home)
        def _():
            drain(xq.at[pl.ds(0, OWN - 1)], rsem.at[1])

        @pl.when(jnp.logical_not(me.home))
        def _():
            drain(xq.at[pl.ds(0, OWN)], rsem.at[1])

        for z in range(4):
            halo(z).start()

        @pl.when(me.home)
        def _():
            drain(xg.at[pl.ds(0, OWN - 1)], rsem.at[2])

        @pl.when(jnp.logical_not(me.home))
        def _():
            drain(xg.at[pl.ds(0, OWN)], rsem.at[2])

        swap().wait()
        for z in range(4):
            halo(z).wait()

    for n, src in enumerate((k_ref, v_ref, q_ref, g_ref)):
        @pl.when(me.home)
        def _():
            drain(src.at[:, pl.ds(0, (HEADS - 1) * D)], ssem.at[n])

        @pl.when(jnp.logical_not(me.home))
        def _():
            drain(src, ssem.at[n])


def collect(q, k, v, g):
    anywhere = pl.BlockSpec(memory_space=pl.ANY)
    return pl.pallas_call(
        collect_kernel,
        out_shape=(
            jax.ShapeDtypeStruct((2, OWN, 2, PIECE, D), BF16),
            jax.ShapeDtypeStruct((OWN, PIECE, D), BF16),
            jax.ShapeDtypeStruct((OWN, PIECE, D), BF16),
            jax.ShapeDtypeStruct((4, PIECE, D), BF16),
        ),
        in_specs=[anywhere] * 4,
        out_specs=(anywhere,) * 4,
        scratch_shapes=[
            pltpu.SemaphoreType.DMA((4,)),
            pltpu.SemaphoreType.DMA((3,)),
            pltpu.SemaphoreType.DMA((4,)),
            pltpu.SemaphoreType.DMA((5,)),
            pltpu.SemaphoreType.DMA((5,)),
        ],
        compiler_params=pltpu.CompilerParams(collective_id=0, has_side_effects=True),
        name="collect",
    )(q, k, v, g)


def head_body(
    core, len_ref, kv_ref, q_ref, g_ref, halo_ref, taps_ref,
    att_ref, own_ref, other_ref, edge_ref,
    stage, hit1, hit2, qc, kc, vc, go, kt, vt, gt, sc, dq, dk, dv,
):
    starts = [jnp.int32(0)]
    for i in range(DOCS - 1):
        starts.append(starts[-1] + len_ref[i])

    def start_of(pos):
        best = jnp.zeros_like(pos)
        for s in starts[1:]:
            best = jnp.where(pos >= s, s, best)
        return best

    def base_of(c, z):
        return pl.multiple_of((z * 2 + lax.rem(z + c, 2)) * BLOCK, BLOCK)

    for a in range(3):
        stage[a, 0:8, :] = jnp.zeros((8, D), F32)

    def unpack(z, _):
        for c in range(2):
            base = base_of(c, z)
            for j in range(PER_BLOCK):
                row = base + j * PIECE
                for a in range(2):
                    stage[1 + a, pl.ds(row + 8, PIECE), :] = kv_ref[c, z * PER_BLOCK + j, a].astype(F32)
        base = base_of(core, z)
        for j in range(PER_BLOCK):
            stage[0, pl.ds(base + j * PIECE + 8, PIECE), :] = q_ref[z * PER_BLOCK + j].astype(F32)
            dq[pl.ds(base + j * PIECE, PIECE), :] = g_ref[z * PER_BLOCK + j].astype(F32)
        stage[0, pl.ds(base_of(1 - core, z) + BLOCK - PIECE + 8, PIECE), :] = halo_ref[z].astype(F32)
        return 0

    lax.fori_loop(0, 4, unpack, 0)

    def mixed(a, base, rows):
        x0 = stage[a, pl.ds(base + 8, rows), :]
        x1 = stage[a, pl.ds(base + 7, rows), :]
        x2 = stage[a, pl.ds(base + 6, rows), :]
        mix = taps_ref[3 * a : 3 * a + 1, :] * x0 + taps_ref[3 * a + 1 : 3 * a + 2, :] * (x1 * hit1[pl.ds(base, rows), :])
        return mix + taps_ref[3 * a + 2 : 3 * a + 3, :] * (x2 * hit2[pl.ds(base, rows), :])

    def keys(i, _):
        base = pl.multiple_of(i * 256, 256)
        pos = base + lax.broadcasted_iota(jnp.int32, (256, 1), 0)
        since = pos - start_of(pos)
        hit1[pl.ds(base, 256), :] = jnp.broadcast_to(jnp.where(since >= 1, 1.0, 0.0).astype(F32), (256, D))
        hit2[pl.ds(base, 256), :] = jnp.broadcast_to(jnp.where(since >= 2, 1.0, 0.0).astype(F32), (256, D))
        for a, dst, dst_t in ((1, kc, kt), (2, vc, vt)):
            mix = mixed(a, base, 256)
            dst[pl.ds(base, 256), :] = mix.astype(BF16)
            dst_t[:, pl.ds(base, 256)] = mix.T.astype(BF16)
        return 0

    lax.fori_loop(0, T // 256, keys, 0)

    def own(z, _):
        base = base_of(core, z)
        qc[pl.ds(base, BLOCK), :] = mixed(0, base, BLOCK).astype(BF16)
        g = dq[pl.ds(base, BLOCK), :]
        go[pl.ds(base, BLOCK), :] = g.astype(BF16)
        gt[:, pl.ds(base, BLOCK)] = g.T
        return 0

    lax.fori_loop(0, 4, own, 0)

    for ref in (dq, dk, dv):
        ref[...] = jnp.zeros(ref.shape, F32)
    for ref in (hit1, hit2):
        ref[T:, :] = jnp.zeros((8, D), F32)

    def queries(z, _):
        t0 = base_of(core, z)
        q = qc[pl.ds(t0, BQ), :]
        g = go[pl.ds(t0, BQ), :]
        tpos = t0 + lax.broadcasted_iota(jnp.int32, (1, BQ), 1)
        tstart = start_of(tpos)
        first = start_of(t0) // BK
        last = (t0 + BQ + BK - 1) // BK
        uio = lax.broadcasted_iota(jnp.int32, (BK, BQ), 0)

        def score(j, m):
            u0 = pl.multiple_of(j * BK, BK)
            s = lax.dot_general(kc[pl.ds(u0, BK), :], q, NT, preferred_element_type=F32)
            s = jnp.where((uio <= tpos - u0) & (uio >= tstart - u0), s, MASKED)
            sc[pl.ds(u0, BK), :] = s
            return jnp.maximum(m, jnp.max(s, axis=0, keepdims=True))

        m = lax.fori_loop(first, last, score, jnp.full((1, BQ), MASKED, F32))
        shift = m * (SCALE * LOG2E)

        def weigh(j, carry):
            total, o = carry
            u0 = pl.multiple_of(j * BK, BK)
            p = jnp.exp2(sc[pl.ds(u0, BK), :] * (SCALE * LOG2E) - shift)
            sc[pl.ds(u0, BK), :] = p
            total = total + jnp.sum(p, axis=0, keepdims=True)
            o = o + dot(vt[:, pl.ds(u0, BK)], p.astype(BF16))
            return total, o

        total, o = lax.fori_loop(first, last, weigh, (jnp.zeros((1, BQ), F32), jnp.zeros((D, BQ), F32)))
        inv = 1.0 / total
        o = o * inv
        delta = jnp.sum(gt[:, pl.ds(t0, BQ)] * o, axis=0, keepdims=True)
        stage[0, pl.ds(t0 + 8, BQ), :] = o.T

        def grads(j, acc):
            u0 = pl.multiple_of(j * BK, BK)
            p = sc[pl.ds(u0, BK), :] * inv
            dp = lax.dot_general(vc[pl.ds(u0, BK), :], g, NT, preferred_element_type=F32)
            ds = (p * (dp - delta)).astype(BF16)
            dk[pl.ds(u0, BK), :] += dot(ds, q)
            dv[pl.ds(u0, BK), :] += dot(p.astype(BF16), g)
            return acc + dot(kt[:, pl.ds(u0, BK)], ds)

        acc = lax.fori_loop(first, last, grads, jnp.zeros((D, BQ), F32))
        dq[pl.ds(t0, BQ), :] = acc.T
        return 0

    lax.fori_loop(0, 4, queries, 0)

    taps = [taps_ref[n : n + 1, :] * (SCALE if n < 6 else 1.0) for n in range(9)]

    def back(a, src, row):
        row = pl.multiple_of(row, 8)
        out = taps[3 * a] * src[pl.ds(row, PIECE), :]
        out = out + taps[3 * a + 1] * (src[pl.ds(row + 1, PIECE), :] * hit1[pl.ds(row + 1, PIECE), :])
        return out + taps[3 * a + 2] * (src[pl.ds(row + 2, PIECE), :] * hit2[pl.ds(row + 2, PIECE), :])

    def finish(z, _):
        base, across = base_of(core, z), base_of(1 - core, z)
        for j in range(PER_BLOCK):
            row, at = base + j * PIECE, z * PER_BLOCK + j
            att_ref[at] = stage[0, pl.ds(pl.multiple_of(row + 8, 8), PIECE), :].astype(BF16)
            own_ref[at, 0] = back(0, dq, row)
            own_ref[at, 1] = back(1, dk, row)
            own_ref[at, 2] = back(2, dv, row)
            row = across + j * PIECE
            other_ref[at, 0] = back(1, dk, row).astype(BF16)
            other_ref[at, 1] = back(2, dv, row).astype(BF16)
        edge_ref[z] = back(0, dq, across + BLOCK - PIECE).astype(BF16)
        return 0

    lax.fori_loop(0, 4, finish, 0)


def head_kernel(*refs):
    me = Place()

    @pl.when(me.owner)
    def _():
        head_body(me.core, *refs)


def one_head(lengths, xkv, xq, xg, xh, taps, kernel=head_kernel):
    vmem = pl.BlockSpec(memory_space=pltpu.VMEM)
    row = functools.partial(pltpu.VMEM, (T + 8, D))
    return pl.pallas_call(
        kernel,
        out_shape=(
            jax.ShapeDtypeStruct((OWN, PIECE, D), BF16),
            jax.ShapeDtypeStruct((OWN, 3, PIECE, D), F32),
            jax.ShapeDtypeStruct((OWN, 2, PIECE, D), BF16),
            jax.ShapeDtypeStruct((4, PIECE, D), BF16),
        ),
        in_specs=[pl.BlockSpec(memory_space=pltpu.SMEM)] + [vmem] * 5,
        out_specs=(vmem,) * 4,
        scratch_shapes=[
            pltpu.VMEM((3, T + 8, D), F32), row(F32), row(F32),
            pltpu.VMEM((T, D), BF16), pltpu.VMEM((T, D), BF16), pltpu.VMEM((T, D), BF16), pltpu.VMEM((T, D), BF16),
            pltpu.VMEM((D, T), BF16), pltpu.VMEM((D, T), BF16), pltpu.VMEM((D, T), F32),
            pltpu.VMEM((T, BQ), F32),
            row(F32), row(F32), row(F32),
        ],
        compiler_params=pltpu.CompilerParams(vmem_limit_bytes=48 << 20),
        name="one_head",
    )(lengths, xkv, xq, xg, xh, taps)


def spread_kernel(att, own, other, edge, out, buf, got, corner, ssem, rsem, lsem, psem, tsem):
    me = Place()
    barrier = pltpu.get_barrier_semaphore()
    @pl.when(me.home)
    def _():
        signal(barrier, me.sibling())

    @pl.when(jnp.logical_not(me.home))
    def _():
        signal(barrier, me.head_at(0)[1])

    def greet(i, _):
        signal(barrier, me.head_at(i)[1])
        return 0

    lax.fori_loop(1, HEADS, greet, 0)
    head = (me.x * 2 + me.yh) * 4 + me.z
    mine = columns(head)

    def swaps():
        return (
            remote(other, got, psem.at[0], tsem.at[0], me.sibling()),
            remote(edge, corner, psem.at[1], tsem.at[1], me.sibling()),
        )

    def send(part, i):
        s, device = me.token_at(i)
        remote(buf.at[s, part], out.at[part, :, mine], ssem, rsem, device).start()

    def keep(part, n):
        s, _ = me.token_at(0)
        return pltpu.make_async_copy(buf.at[s, part], out.at[part, :, mine], lsem.at[n])

    first, rest = pl.ds(0, 1), pl.ds(1, 3)

    def fill_att(i):
        s, _ = me.token_at(i)
        buf[s, 0] = att[s]

    def fill_rest(i):
        s, _ = me.token_at(i)
        buf[s, 1] = (own[s, 0] + jnp.where(lax.rem(s, PER_BLOCK) == PER_BLOCK - 1, corner[s // PER_BLOCK].astype(F32), 0.0)).astype(BF16)
        buf[s, 2] = (own[s, 1] + got[s, 0].astype(F32)).astype(BF16)
        buf[s, 3] = (own[s, 2] + got[s, 1].astype(F32)).astype(BF16)

    @pl.when(me.owner)
    def _():
        @pl.when(me.home)
        def _():
            pl.semaphore_wait(barrier, OWN - 1)

        @pl.when(jnp.logical_not(me.home))
        def _():
            pl.semaphore_wait(barrier, OWN + 1)

        for copy in swaps():
            copy.start()

        for part, fill, n in ((first, fill_att, 0), (rest, fill_rest, 1)):
            if n == 1:
                for copy in swaps():
                    copy.wait()
            fill(0)

            @pl.when(me.home)
            def _():
                keep(part, n).start()

            @pl.when(jnp.logical_not(me.home))
            def _():
                send(part, 0)

            def step(i, _, part=part, fill=fill):
                fill(i)
                send(part, i)
                return 0

            lax.fori_loop(1, OWN, step, 0)

        @pl.when(me.home)
        def _():
            keep(first, 0).wait()
            keep(rest, 1).wait()
            drain(buf.at[pl.ds(0, OWN - 1)], ssem)

        @pl.when(jnp.logical_not(me.home))
        def _():
            drain(buf, ssem)

    @pl.when(me.home)
    def _():
        drain(out.at[:, :, pl.ds(0, (HEADS - 1) * D)], rsem)

    @pl.when(jnp.logical_not(me.home))
    def _():
        drain(out, rsem)


def spread(att, own, other, edge):
    vmem = pl.BlockSpec(memory_space=pltpu.VMEM)
    return pl.pallas_call(
        spread_kernel,
        out_shape=jax.ShapeDtypeStruct((4, PIECE, HEADS * D), BF16),
        in_specs=[vmem] * 4,
        out_specs=pl.BlockSpec(memory_space=pl.ANY),
        scratch_shapes=[
            pltpu.VMEM((OWN, 4, PIECE, D), BF16),
            pltpu.VMEM((OWN, 2, PIECE, D), BF16),
            pltpu.VMEM((4, PIECE, D), BF16),
            pltpu.SemaphoreType.DMA,
            pltpu.SemaphoreType.DMA,
            pltpu.SemaphoreType.DMA((2,)),
            pltpu.SemaphoreType.DMA((2,)),
            pltpu.SemaphoreType.DMA((2,)),
        ],
        compiler_params=pltpu.CompilerParams(collective_id=1, has_side_effects=True),
        name="spread",
    )(att, own, other, edge)


def on_device(query_in, key_in, value_in, grad_out, kernel, lengths):
    own_head = kernel.reshape(9, 4, D)
    taps = lax.dynamic_index_in_dim(own_head, lax.axis_index("z"), 1, keepdims=False)
    xkv, xq, xg, xh = collect(query_in, key_in, value_in, grad_out)
    out = spread(*one_head(lengths, xkv, xq, xg, xh, taps))
    return tuple(out[i] for i in range(4))


def solution(mesh):
    fine = Mesh(mesh.devices.reshape(SIZES), NAMES)
    rows = P(NAMES, None)
    return jax.shard_map(
        on_device,
        mesh=fine,
        in_specs=(rows, rows, rows, rows, P(None, None, ("x", "yh")), P()),
        out_specs=(rows,) * 4,
        check_vma=False,
    )
```

time: 291 us -> 91.8 us (0.32); the launches traced: 286 us -> 91.4 us
  waiting for transfers between devices: 88.1 us -> 0 us
  Pallas kernels: 0 us -> 79.4 us
  blocking collectives: 69.2 us -> 0 us
  matrix products: 36.1 us -> 0 us
  starting transfers between devices: 29.6 us -> 0 us
  local copies, waits for them, and re-layouts: 38.4 us -> 11.3 us
  between operations: 14.1 us -> 0.7 us
  other arithmetic: 10.4 us -> 0 us
    pallas_call x0 -> x3, Pallas kernels: none -> 79.4 us  [the longest x1 32.6 us: collect(): pl.pallas_call(collect_kernel, out_shape=(jax.ShapeDtypeStruct((2, OWN, 2...]
    all_gather x4 -> x0, waiting for transfers between devices: 59.3 us -> none  [the longest x1 35.1 us: on_device(): value_piece = lax.all_gather(value_conv, 'seq', axis=0, tiled=True)]
    dot_general x6 -> x0, matrix products: 36.1 us -> none  [the longest x1 10.3 us: on_device(): jnp.einsum('hqk,khd->qhd', dscores, split_heads(key_piece), preferred_ele...]
    all_gather x2 -> x0, blocking collectives: 35.2 us -> none  [the longest x1 18.5 us: on_device(): lax.all_gather(delta_rows, 'seq', axis=0, tiled=True)]
    all_to_all x3 -> x0, blocking collectives: 34 us -> none  [the longest x1 14.5 us: on_device(): lax.all_to_all(grad_out, 'head', split_axis=1, concat_axis=0, tiled=True)]
    all_to_all x5 -> x0, waiting for transfers between devices: 27.6 us -> none  [the longest x1 7.01 us: on_device(): lax.all_to_all(query_in, 'head', split_axis=1, concat_axis=0, tiled=True)]
    all_to_all x5 -> x0, starting transfers between devices: 20.2 us -> none  [the longest x1 6.21 us: on_device(): lax.all_to_all(attended_out, 'head', split_axis=0, concat_axis=1, tiled=T...]
    all_gather x6 -> x0, local copies, waits for them, and re-layouts: 15.7 us -> none  [the longest x1 4.73 us: on_device(): grad_piece = lax.all_gather(grad_rows, 'seq', axis=0, tiled=True)]
  transfers between devices with their start and end apart: 11 -> 0, of which waited for: 8 -> 0; matrix products, arithmetic and copies ran while one was open for 22% -> 0% of each run, Pallas kernels for 0% -> 0%
where the time goes in v1:
time: 91.8 us; the launch traced here: 91.4 us
  Pallas kernels  79.4 us (86%)
  local copies, waits for them, and re-layouts  11.3 us (12%)
    pallas_call x1, Pallas kernels, collect(): pl.pallas_call(collect_kernel, out_shape=(jax.ShapeDtypeStruct((2, OWN, 2...  32.6 us
    pallas_call x1, Pallas kernels, spread(): pl.pallas_call(spread_kernel, out_shape=jax.ShapeDtypeStruct((4, PIECE, H...  25.8 us
    pallas_call x1, Pallas kernels, one_head(): pl.pallas_call(kernel, out_shape=(jax.ShapeDtypeStruct((OWN, PIECE, D), B...  21.1 us
    unnamed x19, local copies, waits for them, and re-layouts  8.42 us
    squeeze x1, local copies, waits for them, and re-layouts, on_device(): return tuple((out[i] for i in range(4)))  2.11 us

profile of v1, /device:TPU:1, one launch (start us, length us, event | category | flops | bytes accessed | tf_op | source)
XLA Modules:
  0.0 91.4 jit_solution(2243802197994532644)
XLA Ops:
  0.6 0.8 reshape.11
  1.4 32.6 %collect.1 = (bf16[2,64,2,24,128]{4,3,2,1,0:T(8,128)(2,1)}, bf16[64,24,128]{2,1,0:T(8,128)(2,1)}, bf16[64,24,128]{2,1,0:T(8,128)(2,1)}, bf16[4,24,128]{2,1,0:T(8,128)(2,1)}) custom-call(bf16[24,4096]{1,0:T(8,128)(2,1)} %q_ref.1, bf16[24,4096]{1,0:T(8,128)(2,1)} %k_ref.1, bf16[24,4096]{1,0:T(8,128)(2,1)} %v_ref.1, bf16[24,4096]{1,0:T(8,128)(2,1)} %g_ref.1), custom_call_target="tpu_custom_call" | custom-call | tf_op jit(solution)/shard_map/collect/pallas_call | solution.py:179
  34.0 0.0 copy-start.1
  34.0 1.4 %copy-done.1 = bf16[2,64,2,24,128]{4,3,2,1,0:T(8,128)(2,1)S(1)} copy-done((bf16[2,64,2,24,128]{4,3,2,1,0:T(8,128)(2,1)S(1)}, bf16[2,64,2,24,128]{4,3,2,1,0:T(8,128)(2,1)}, u32[]{:S(2)}) %copy-start.1) | copy-done | bytes 1572888
  35.4 0.0 copy-start.4
  35.4 1.0 %copy-done.4 = bf16[64,24,128]{2,1,0:T(8,128)(2,1)S(1)} copy-done((bf16[64,24,128]{2,1,0:T(8,128)(2,1)S(1)}, bf16[64,24,128]{2,1,0:T(8,128)(2,1)}, u32[]{:S(2)}) %copy-start.4) | copy-done | bytes 393240
  36.4 0.0 copy-start.5
  36.4 1.0 %copy-done.5 = bf16[64,24,128]{2,1,0:T(8,128)(2,1)S(1)} copy-done((bf16[64,24,128]{2,1,0:T(8,128)(2,1)S(1)}, bf16[64,24,128]{2,1,0:T(8,128)(2,1)}, u32[]{:S(2)}) %copy-start.5) | copy-done | bytes 393240
  37.4 0.0 copy-start.6
  37.4 0.7 copy-done.6
  38.1 0.0 copy-start.8
  38.1 0.7 copy-done.8
  38.8 21.1 %one_head.1 = (bf16[64,24,128]{2,1,0:T(8,128)(2,1)S(1)}, f32[64,3,24,128]{3,2,1,0:T(8,128)S(1)}, bf16[64,2,24,128]{3,2,1,0:T(8,128)(2,1)S(1)}, bf16[4,24,128]{2,1,0:T(8,128)(2,1)S(1)}) custom-call(s32[12]{0:T(128)S(1)} %copy-done.8, bf16[2,64,2,24,128]{4,3,2,1,0:T(8,128)(2,1)S(1)} %copy-done.1, bf16[64,24,128]{2,1,0:T(8,128)(2,1)S(1)} %copy-done.4, ...), custom_call_target="tpu_custom_call" | custom-call | tf_op jit(solution)/shard_map/one_head/pallas_call | solution.py:360
  59.9 0.0 copy-start
  59.9 1.4 %copy-done = f32[64,3,24,128]{3,2,1,0:T(8,128)} copy-done((f32[64,3,24,128]{3,2,1,0:T(8,128)}, f32[64,3,24,128]{3,2,1,0:T(8,128)S(1)}, u32[]{:S(2)}) %copy-start) | copy-done | bytes 2359320
  61.3 0.0 copy-start.2
  61.3 0.9 copy-done.2
  62.2 0.0 copy-start.3
  62.2 0.7 copy-done.3
  62.9 0.0 copy-start.7
  62.9 0.6 copy-done.7
  63.5 25.8 %spread.1 = bf16[4,24,4096]{2,1,0:T(8,128)(2,1)} custom-call(bf16[64,24,128]{2,1,0:T(8,128)(2,1)} %copy-done.3, f32[64,3,24,128]{3,2,1,0:T(8,128)} %copy-done, bf16[64,2,24,128]{3,2,1,0:T(8,128)(2,1)} %copy-done.2, bf16[4,24,128]{2,1,0:T(8,128)(2,1)} %copy-done.7), custom_call_target="tpu_custom_call" | custom-call | tf_op jit(solution)/shard_map/spread/pallas_call | solution.py:482
  89.3 2.1 %slice_bitcast_fusion = (bf16[24,4096]{1,0:T(8,128)(2,1)}, bf16[24,4096]{1,0:T(8,128)(2,1)}, bf16[24,4096]{1,0:T(8,128)(2,1)}, bf16[24,4096]{1,0:T(8,128)(2,1)}) fusion(bf16[4,24,4096]{2,1,0:T(8,128)(2,1)} %spread.1), kind=kLoop, calls=%fused_computation | loop fusion | bytes 1572864 | tf_op jit(solution)/shard_map/squeeze | solution.py:507
  (2 shorter events, 0.0 us)
Async XLA Ops:
  34.0 1.4 %copy-start.1 = (bf16[2,64,2,24,128]{4,3,2,1,0:T(8,128)(2,1)S(1)}, bf16[2,64,2,24,128]{4,3,2,1,0:T(8,128)(2,1)}, u32[]{:S(2)}) copy-start(bf16[2,64,2,24,128]{4,3,2,1,0:T(8,128)(2,1)} %get-tuple-element.12.refs_1_) | copy-start | bytes 4718596
  35.4 1.0 %copy-start.4 = (bf16[64,24,128]{2,1,0:T(8,128)(2,1)S(1)}, bf16[64,24,128]{2,1,0:T(8,128)(2,1)}, u32[]{:S(2)}) copy-start(bf16[64,24,128]{2,1,0:T(8,128)(2,1)} %get-tuple-element.13.refs_2_) | copy-start | bytes 1179652
  36.4 1.0 %copy-start.5 = (bf16[64,24,128]{2,1,0:T(8,128)(2,1)S(1)}, bf16[64,24,128]{2,1,0:T(8,128)(2,1)}, u32[]{:S(2)}) copy-start(bf16[64,24,128]{2,1,0:T(8,128)(2,1)} %get-tuple-element.14.refs_3_) | copy-start | bytes 1179652
  37.4 0.7 copy-start.6
  38.1 0.7 copy-start.8
  59.9 1.4 %copy-start = (f32[64,3,24,128]{3,2,1,0:T(8,128)}, f32[64,3,24,128]{3,2,1,0:T(8,128)S(1)}, u32[]{:S(2)}) copy-start(f32[64,3,24,128]{3,2,1,0:T(8,128)S(1)} %get-tuple-element.17.own) | copy-start | bytes 7077892
  61.3 0.9 copy-start.2
  62.2 0.7 copy-start.3
  62.9 0.6 copy-start.7

commit v2 on v1

v2 whole, which is shorter than its diff:
```python
import functools

import jax
import jax.numpy as jnp
from jax import lax
from jax.experimental import pallas as pl
from jax.experimental.pallas import tpu as pltpu
from jax.sharding import Mesh
from jax.sharding import PartitionSpec as P

NAMES = ("z", "yl", "core", "x", "yh")
SIZES = (4, 2, 2, 4, 2)
D = 128
T = 3072
HEADS = 32
PIECE = 24
BLOCK = 384
PER_BLOCK = BLOCK // PIECE
OWN = 32
DOCS = 12
BQ = BLOCK
BK = 768
MASKED = -1.0e30
SCALE = D**-0.5
LOG2E = 1.4426950408889634
NT = (((1,), (1,)), ((), ()))
F32, BF16 = jnp.float32, jnp.bfloat16
MESH = pl.DeviceIdType.MESH


def dot(a, b):
    return jnp.dot(a, b, preferred_element_type=F32)


class Place:
    def __init__(self):
        self.z, self.yl, self.core, self.x, self.yh = (lax.axis_index(n) for n in NAMES)
        self.zbit = lax.rem(self.z, 2)
        self.head = (self.x * 2 + self.yh) * 4 + self.z
        self.slot = self.z // 2 * PER_BLOCK + self.core * 8 + self.x * 2 + self.yh
        self.side = jnp.where(self.zbit == self.yl, 0, 1)
        self.near = self.core == self.yl
        self.home = self.near & (self.side == 0)
        self.quarter = self.yl * 2 + self.core

    def owner_at(self, i, chip):
        k = lax.rem(i + self.head, HEADS)
        return k, dict(z=lax.rem(k, 4), yl=chip, core=self.yl, x=k // 8, yh=lax.rem(k // 4, 2))

    def token_at(self, i, side):
        s = lax.rem(i + self.slot, OWN)
        z = s // PER_BLOCK * 2 + lax.rem(self.yl + side, 2)
        return s, dict(z=z, yl=self.core, core=lax.rem(s // 8, 2), x=lax.rem(s // 2, 4), yh=lax.rem(s, 2))

    def other(self, yl, core):
        return dict(z=self.z, yl=yl, core=core, x=self.x, yh=self.yh)

    def sibling(self):
        return self.other(self.yl, 1 - self.core)

    def quarter_at(self, step):
        q = lax.rem(self.quarter + step + 4, 4)
        return self.other(q // 2, lax.rem(q, 2))


def signal(sem, device):
    pl.semaphore_signal(sem, 1, device_id=device, device_id_type=MESH)


def remote(src, dst, send, recv, device):
    return pltpu.make_async_remote_copy(src, dst, send, recv, device_id=device, device_id_type=MESH)


def drain(ref, sem):
    pltpu.make_async_copy(ref, ref, sem).wait()


def columns(head):
    return pl.ds(pl.multiple_of(head * D, D), D)


def settle(fewer, ref, part, sem):
    @pl.when(fewer)
    def _():
        drain(part, sem)

    @pl.when(jnp.logical_not(fewer))
    def _():
        drain(ref, sem)


def either(here, local, away):
    pl.when(here)(local)
    pl.when(jnp.logical_not(here))(away)


def most(ref):
    return ref.at[:, :, pl.ds(0, (HEADS - 1) * D)]


def collect_kernel(q_ref, k_ref, v_ref, g_ref, xkv, ykv, xqg, xh, buf, load, ssem, rsem, lsem, psem, tsem):
    me = Place()
    loads = [pltpu.make_async_copy(src, buf.at[n], load.at[n]) for n, src in enumerate((k_ref, v_ref, q_ref, g_ref))]
    for copy in loads:
        copy.start()

    barrier = pltpu.get_barrier_semaphore()
    signal(barrier, me.sibling())
    signal(barrier, me.quarter_at(-1))
    for side in range(2):
        @pl.when(jnp.logical_not(me.near & (me.side == side)))
        def _():
            signal(barrier, me.token_at(0, side)[1])

    def greet(i, _):
        for side in range(2):
            signal(barrier, me.token_at(i, side)[1])
        return 0

    lax.fori_loop(1, OWN, greet, 0)
    for copy in loads:
        copy.wait()
    either(
        me.near,
        lambda: pl.semaphore_wait(barrier, 2 * HEADS + 1),
        lambda: pl.semaphore_wait(barrier, 2 * HEADS + 2),
    )

    kv, qg = buf.at[pl.ds(0, 2)], buf.at[pl.ds(2, 2)]

    def side_at(chip):
        return jnp.where(me.zbit == chip, 0, 1)

    def send_kv(i, chip):
        head, device = me.owner_at(i, chip)
        side = side_at(chip)
        remote(kv.at[:, :, columns(head)], xkv.at[side, me.slot], ssem.at[chip], rsem.at[side], device).start()

    def send_qg(i):
        head, device = me.owner_at(i, me.zbit)
        remote(qg.at[:, :, columns(head)], xqg.at[me.slot], ssem.at[2], rsem.at[2], device).start()

    def keep_kv():
        return pltpu.make_async_copy(kv.at[:, :, columns(me.head)], xkv.at[me.side, me.slot], lsem.at[0])

    def keep_qg():
        return pltpu.make_async_copy(qg.at[:, :, columns(me.head)], xqg.at[me.slot], lsem.at[1])

    for chip in range(2):
        either(me.near & (me.yl == chip), lambda: keep_kv().start(), lambda: send_kv(0, chip))

    def all_kv(i, _):
        send_kv(i, 0)
        send_kv(i, 1)
        return 0

    lax.fori_loop(1, HEADS, all_kv, 0)
    either(me.home, lambda: keep_qg().start(), lambda: send_qg(0))

    def all_qg(i, _):
        send_qg(i)
        return 0

    lax.fori_loop(1, HEADS, all_qg, 0)

    swap = remote(xkv, ykv, psem.at[0], tsem.at[0], me.sibling())
    halos = [
        remote(xqg.at[i * PER_BLOCK + PER_BLOCK - 1, 0], xh.at[i], psem.at[1 + i], tsem.at[1 + i], me.quarter_at(1))
        for i in range(2)
    ]
    for side in range(2):
        settle(me.near & (me.side == side), xkv.at[side], xkv.at[side, pl.ds(0, OWN - 1)], rsem.at[side])
    pl.when(me.near)(lambda: keep_kv().wait())
    swap.start()
    settle(me.home, xqg, xqg.at[pl.ds(0, OWN - 1)], rsem.at[2])
    pl.when(me.home)(lambda: keep_qg().wait())
    for copy in halos:
        copy.start()
    for chip in range(2):
        settle(me.near & (me.yl == chip), kv, most(kv), ssem.at[chip])
    settle(me.home, qg, most(qg), ssem.at[2])
    swap.wait()
    for copy in halos:
        copy.wait()


def collect(q, k, v, g):
    hbm, anywhere = pl.BlockSpec(memory_space=pltpu.HBM), pl.BlockSpec(memory_space=pl.ANY)
    return pl.pallas_call(
        collect_kernel,
        out_shape=(
            pltpu.VMEM((2, OWN, 2, PIECE, D), BF16),
            pltpu.VMEM((2, OWN, 2, PIECE, D), BF16),
            pltpu.VMEM((OWN, 2, PIECE, D), BF16),
            pltpu.VMEM((2, PIECE, D), BF16),
        ),
        in_specs=[hbm] * 4,
        out_specs=(anywhere,) * 4,
        scratch_shapes=[
            pltpu.VMEM((4, PIECE, HEADS * D), BF16),
            pltpu.SemaphoreType.DMA((4,)),
            pltpu.SemaphoreType.DMA((3,)),
            pltpu.SemaphoreType.DMA((3,)),
            pltpu.SemaphoreType.DMA((2,)),
            pltpu.SemaphoreType.DMA((3,)),
            pltpu.SemaphoreType.DMA((3,)),
        ],
        compiler_params=pltpu.CompilerParams(collective_id=0, has_side_effects=True, vmem_limit_bytes=16 << 20),
        name="collect",
    )(*(pltpu.with_memory_space_constraint(x, pltpu.HBM) for x in (q, k, v, g)))


def head_body(
    yl, core, lane, len_ref, kv_ref, kv_other, qg_ref, halo_ref, all_taps,
    att_ref, dq_ref, own_ref, other_ref, edge_ref,
    stage, hit1, hit2, qc, kc, vc, go, kt, vt, gt, sc, dq, dk, dv,
):
    starts = [jnp.int32(0)]
    for i in range(DOCS - 1):
        starts.append(starts[-1] + len_ref[i])

    def start_of(pos):
        best = jnp.zeros_like(pos)
        for s in starts[1:]:
            best = jnp.where(pos >= s, s, best)
        return best

    def tap(n):
        return all_taps[n // 3, n % 3 : n % 3 + 1, pl.ds(pl.multiple_of(lane * D, D), D)]

    quarter = yl * 2 + core
    before = lax.rem(quarter + 3, 4)

    def base_of(q, i):
        return pl.multiple_of((q + 4 * i) * BLOCK, BLOCK)

    sides = [(kv, side, lax.rem(yl + side, 2) * 2 + c) for kv, c in ((kv_ref, core), (kv_other, 1 - core)) for side in range(2)]
    for a in range(3):
        stage[a, 0:8, :] = jnp.zeros((8, D), F32)

    def unpack(i, _):
        for kv, side, q in sides:
            base = base_of(q, i)
            for j in range(PER_BLOCK):
                for a in range(2):
                    stage[1 + a, pl.ds(base + j * PIECE + 8, PIECE), :] = kv[side, i * PER_BLOCK + j, a].astype(F32)
        base = base_of(quarter, i)
        for j in range(PER_BLOCK):
            stage[0, pl.ds(base + j * PIECE + 8, PIECE), :] = qg_ref[i * PER_BLOCK + j, 0].astype(F32)
            dq[pl.ds(base + j * PIECE, PIECE), :] = qg_ref[i * PER_BLOCK + j, 1].astype(F32)
        stage[0, pl.ds(base_of(before, i) + BLOCK - PIECE + 8, PIECE), :] = halo_ref[i].astype(F32)
        return 0

    lax.fori_loop(0, 2, unpack, 0)

    def mixed(a, base, rows):
        x0 = stage[a, pl.ds(base + 8, rows), :]
        x1 = stage[a, pl.ds(base + 7, rows), :]
        x2 = stage[a, pl.ds(base + 6, rows), :]
        mix = tap(3 * a) * x0 + tap(3 * a + 1) * (x1 * hit1[pl.ds(base, rows), :])
        return mix + tap(3 * a + 2) * (x2 * hit2[pl.ds(base, rows), :])

    def keys(i, _):
        base = pl.multiple_of(i * 256, 256)
        pos = base + lax.broadcasted_iota(jnp.int32, (256, 1), 0)
        since = pos - start_of(pos)
        hit1[pl.ds(base, 256), :] = jnp.broadcast_to(jnp.where(since >= 1, 1.0, 0.0).astype(F32), (256, D))
        hit2[pl.ds(base, 256), :] = jnp.broadcast_to(jnp.where(since >= 2, 1.0, 0.0).astype(F32), (256, D))
        for a, dst, dst_t in ((1, kc, kt), (2, vc, vt)):
            mix = mixed(a, base, 256)
            dst[pl.ds(base, 256), :] = mix.astype(BF16)
            dst_t[:, pl.ds(base, 256)] = mix.T.astype(BF16)
        return 0

    lax.fori_loop(0, T // 256, keys, 0)

    def own(i, _):
        base = base_of(quarter, i)
        qc[pl.ds(base, BLOCK), :] = mixed(0, base, BLOCK).astype(BF16)
        g = dq[pl.ds(base, BLOCK), :]
        go[pl.ds(base, BLOCK), :] = g.astype(BF16)
        gt[:, pl.ds(base, BLOCK)] = g.T
        return 0

    lax.fori_loop(0, 2, own, 0)

    for ref in (dq, dk, dv):
        ref[...] = jnp.zeros(ref.shape, F32)
    for ref in (hit1, hit2):
        ref[T:, :] = jnp.zeros((8, D), F32)
    for ref in (kc, vc):
        ref[T:, :] = jnp.zeros((BK, D), BF16)
    for ref in (kt, vt):
        ref[:, T:] = jnp.zeros((D, BK), BF16)

    def queries(i, _):
        t0 = base_of(quarter, i)
        q = qc[pl.ds(t0, BQ), :]
        g = go[pl.ds(t0, BQ), :]
        tpos = t0 + lax.broadcasted_iota(jnp.int32, (1, BQ), 1)
        tstart = start_of(tpos)
        from_row = start_of(t0) // D * D
        tiles = (t0 + BQ - from_row + BK - 1) // BK
        uio = lax.broadcasted_iota(jnp.int32, (BK, BQ), 0)

        def score(j, m):
            u0 = pl.multiple_of(from_row + j * BK, D)
            s = lax.dot_general(kc[pl.ds(u0, BK), :], q, NT, preferred_element_type=F32)
            s = jnp.where((uio <= tpos - u0) & (uio >= tstart - u0), s, MASKED)
            sc[pl.ds(u0, BK), :] = s
            return jnp.maximum(m, jnp.max(s, axis=0, keepdims=True))

        m = lax.fori_loop(0, tiles, score, jnp.full((1, BQ), MASKED, F32))
        shift = m * (SCALE * LOG2E)

        def weigh(j, carry):
            total, o = carry
            u0 = pl.multiple_of(from_row + j * BK, D)
            p = jnp.exp2(sc[pl.ds(u0, BK), :] * (SCALE * LOG2E) - shift)
            sc[pl.ds(u0, BK), :] = p
            total = total + jnp.sum(p, axis=0, keepdims=True)
            o = o + dot(vt[:, pl.ds(u0, BK)], p.astype(BF16))
            return total, o

        total, o = lax.fori_loop(0, tiles, weigh, (jnp.zeros((1, BQ), F32), jnp.zeros((D, BQ), F32)))
        inv = 1.0 / total
        o = o * inv
        delta = jnp.sum(gt[:, pl.ds(t0, BQ)] * o, axis=0, keepdims=True)
        stage[0, pl.ds(t0 + 8, BQ), :] = o.T

        def grads(j, acc):
            u0 = pl.multiple_of(from_row + j * BK, D)
            p = sc[pl.ds(u0, BK), :] * inv
            dp = lax.dot_general(vc[pl.ds(u0, BK), :], g, NT, preferred_element_type=F32)
            ds = (p * (dp - delta)).astype(BF16)
            dk[pl.ds(u0, BK), :] += dot(ds, q)
            dv[pl.ds(u0, BK), :] += dot(p.astype(BF16), g)
            return acc + dot(kt[:, pl.ds(u0, BK)], ds)

        acc = lax.fori_loop(0, tiles, grads, jnp.zeros((D, BQ), F32))
        dq[pl.ds(t0, BQ), :] = acc.T
        return 0

    lax.fori_loop(0, 2, queries, 0)

    taps = [tap(n) * (SCALE if n < 6 else 1.0) for n in range(9)]

    def back(a, src, row):
        row = pl.multiple_of(row, 8)
        out = taps[3 * a] * src[pl.ds(row, PIECE), :]
        out = out + taps[3 * a + 1] * (src[pl.ds(row + 1, PIECE), :] * hit1[pl.ds(row + 1, PIECE), :])
        return out + taps[3 * a + 2] * (src[pl.ds(row + 2, PIECE), :] * hit2[pl.ds(row + 2, PIECE), :])

    def finish(i, _):
        base = base_of(quarter, i)
        for j in range(PER_BLOCK):
            row, at = base + j * PIECE, i * PER_BLOCK + j
            att_ref[at] = stage[0, pl.ds(pl.multiple_of(row + 8, 8), PIECE), :].astype(BF16)
            dq_ref[at] = back(0, dq, row)
        for n, (_, side, q) in enumerate(sides):
            for j in range(PER_BLOCK):
                row, at = base_of(q, i) + j * PIECE, i * PER_BLOCK + j
                if n < 2:
                    own_ref[side, at, 0] = back(1, dk, row)
                    own_ref[side, at, 1] = back(2, dv, row)
                else:
                    other_ref[side, at, 0] = back(1, dk, row).astype(BF16)
                    other_ref[side, at, 1] = back(2, dv, row).astype(BF16)
        edge_ref[i] = back(0, dq, base_of(before, i) + BLOCK - PIECE).astype(BF16)
        return 0

    lax.fori_loop(0, 2, finish, 0)


def head_kernel(*refs):
    head_body(lax.axis_index("yl"), lax.axis_index("core"), lax.axis_index("z"), *refs)


def one_head(lengths, *arrays, kernel=head_kernel):
    vmem = pl.BlockSpec(memory_space=pltpu.VMEM)
    return pl.pallas_call(
        kernel,
        out_shape=(
            pltpu.VMEM((OWN, PIECE, D), BF16),
            pltpu.VMEM((OWN, PIECE, D), F32),
            pltpu.VMEM((2, OWN, 2, PIECE, D), F32),
            pltpu.VMEM((2, OWN, 2, PIECE, D), BF16),
            pltpu.VMEM((2, PIECE, D), BF16),
        ),
        in_specs=[pl.BlockSpec(memory_space=pltpu.SMEM)] + [vmem] * 5,
        out_specs=(vmem,) * 5,
        scratch_shapes=[
            pltpu.VMEM((3, T + 8, D), F32), pltpu.VMEM((T + 8, D), F32), pltpu.VMEM((T + 8, D), F32),
            pltpu.VMEM((T, D), BF16), pltpu.VMEM((T + BK, D), BF16), pltpu.VMEM((T + BK, D), BF16), pltpu.VMEM((T, D), BF16),
            pltpu.VMEM((D, T + BK), BF16), pltpu.VMEM((D, T + BK), BF16), pltpu.VMEM((D, T), F32),
            pltpu.VMEM((T + BK, BQ), F32),
            pltpu.VMEM((T + 8, D), F32), pltpu.VMEM((T + BK, D), F32), pltpu.VMEM((T + BK, D), F32),
        ],
        compiler_params=pltpu.CompilerParams(vmem_limit_bytes=44 << 20),
        name="one_head",
    )(lengths, *arrays)


def spread_kernel(
    att, dq, own, other, edge, out_a, out_k, buf_a, buf_k, got, corner, ssem, rsem, lsem, psem, tsem
):
    me = Place()
    barrier = pltpu.get_barrier_semaphore()
    signal(barrier, me.sibling())
    signal(barrier, me.quarter_at(1))
    for chip in range(2):
        @pl.when(jnp.logical_not(me.near & (me.yl == chip)))
        def _():
            signal(barrier, me.owner_at(0, chip)[1])

    def greet(i, _):
        for chip in range(2):
            signal(barrier, me.owner_at(i, chip)[1])
        return 0

    lax.fori_loop(1, HEADS, greet, 0)
    either(
        me.near,
        lambda: pl.semaphore_wait(barrier, 2 * OWN + 1),
        lambda: pl.semaphore_wait(barrier, 2 * OWN + 2),
    )
    swap = remote(other, got, psem.at[0], tsem.at[0], me.sibling())
    turn = remote(edge, corner, psem.at[1], tsem.at[1], me.quarter_at(-1))
    swap.start()
    turn.start()
    mine = columns(me.head)

    def fill_a(i):
        s, _ = me.token_at(i, 0)
        buf_a[s, 0] = att[s]
        last = lax.rem(s, PER_BLOCK) == PER_BLOCK - 1
        buf_a[s, 1] = (dq[s] + jnp.where(last, corner[s // PER_BLOCK].astype(F32), 0.0)).astype(BF16)

    def send_a(i):
        s, device = me.token_at(i, 0)
        remote(buf_a.at[s], out_a.at[:, :, mine], ssem.at[2], rsem.at[2], device).start()

    def keep_a():
        return pltpu.make_async_copy(buf_a.at[me.slot], out_a.at[:, :, mine], lsem.at[0])

    def fill_k(i):
        s, _ = me.token_at(i, 0)
        for side in range(2):
            buf_k[side, s] = (own[side, s] + got[side, s].astype(F32)).astype(BF16)

    def send_k(i, side):
        s, device = me.token_at(i, side)
        remote(buf_k.at[side, s], out_k.at[side, :, :, mine], ssem.at[side], rsem.at[side], device).start()

    def keep_k(side):
        return pltpu.make_async_copy(buf_k.at[side, me.slot], out_k.at[side, :, :, mine], lsem.at[1])

    turn.wait()
    fill_a(0)
    either(me.home, lambda: keep_a().start(), lambda: send_a(0))

    def all_a(i, _):
        fill_a(i)
        send_a(i)
        return 0

    lax.fori_loop(1, OWN, all_a, 0)
    swap.wait()
    fill_k(0)
    for side in range(2):
        either(me.near & (me.side == side), lambda: keep_k(side).start(), lambda: send_k(0, side))

    def all_k(i, _):
        fill_k(i)
        send_k(i, 0)
        send_k(i, 1)
        return 0

    lax.fori_loop(1, OWN, all_k, 0)
    pl.when(me.home)(lambda: keep_a().wait())
    settle(me.home, out_a, most(out_a), rsem.at[2])
    settle(me.home, buf_a, buf_a.at[pl.ds(0, OWN - 1)], ssem.at[2])
    for side in range(2):
        same = me.near & (me.side == side)
        pl.when(same)(lambda: keep_k(side).wait())
        settle(same, out_k.at[side], most(out_k.at[side]), rsem.at[side])
        settle(same, buf_k.at[side], buf_k.at[side, pl.ds(0, OWN - 1)], ssem.at[side])


def spread(*arrays):
    vmem = pl.BlockSpec(memory_space=pltpu.VMEM)
    return pl.pallas_call(
        spread_kernel,
        out_shape=(pltpu.VMEM((2, PIECE, HEADS * D), BF16), pltpu.VMEM((2, 2, PIECE, HEADS * D), BF16)),
        in_specs=[vmem] * 5,
        out_specs=(pl.BlockSpec(memory_space=pl.ANY),) * 2,
        scratch_shapes=[
            pltpu.VMEM((OWN, 2, PIECE, D), BF16),
            pltpu.VMEM((2, OWN, 2, PIECE, D), BF16),
            pltpu.VMEM((2, OWN, 2, PIECE, D), BF16),
            pltpu.VMEM((2, PIECE, D), BF16),
            pltpu.SemaphoreType.DMA((3,)),
            pltpu.SemaphoreType.DMA((3,)),
            pltpu.SemaphoreType.DMA((2,)),
            pltpu.SemaphoreType.DMA((2,)),
            pltpu.SemaphoreType.DMA((2,)),
        ],
        compiler_params=pltpu.CompilerParams(collective_id=1, has_side_effects=True, vmem_limit_bytes=32 << 20),
        name="spread",
    )(*arrays)


def on_device(query_in, key_in, value_in, grad_out, kernel, lengths):
    xkv, ykv, xqg, xh = collect(query_in, key_in, value_in, grad_out)
    plain, parts = spread(*one_head(lengths, xkv, ykv, xqg, xh, kernel))
    summed = (parts[0].astype(F32) + parts[1].astype(F32)).astype(BF16)
    return plain[0], plain[1], summed[0], summed[1]


def solution(mesh):
    fine = Mesh(mesh.devices.reshape(SIZES), NAMES)
    rows = P(NAMES, None)
    return jax.shard_map(
        on_device,
        mesh=fine,
        in_specs=(rows, rows, rows, rows, P(None, None, ("x", "yh")), P()),
        out_specs=(rows,) * 4,
        check_vma=False,
    )
```

time: 91.8 us -> 74.6 us (0.81)
  Pallas kernels: 79.4 us -> 70.7 us
  local copies, waits for them, and re-layouts: 11.3 us -> 2.92 us
    pallas_call x3, Pallas kernels: 79.4 us -> 70.7 us  [the longest x1 32.8 us: collect(): pl.pallas_call(collect_kernel, out_shape=(pltpu.VMEM((2, OWN, 2, PIECE, D...]
    unnamed x19 -> x4, local copies, waits for them, and re-layouts: 8.42 us -> 1.39 us
    squeeze x1 -> x2, local copies, waits for them, and re-layouts: 2.11 us -> 1.54 us  [on_device(): return (plain[0], plain[1], summed[0], summed[1])]
where the time goes in v2:
time: 74.6 us; the launch traced here: 74.4 us
  Pallas kernels  70.7 us (95%)
  local copies, waits for them, and re-layouts  2.92 us (4%)
    pallas_call x1, Pallas kernels, collect(): pl.pallas_call(collect_kernel, out_shape=(pltpu.VMEM((2, OWN, 2, PIECE, D...  32.8 us
    pallas_call x1, Pallas kernels, spread(): pl.pallas_call(spread_kernel, out_shape=(pltpu.VMEM((2, PIECE, HEADS * D)...  28.2 us
    pallas_call x1, Pallas kernels, one_head(): pl.pallas_call(kernel, out_shape=(pltpu.VMEM((OWN, PIECE, D), BF16), pltp...  9.81 us
    squeeze x2, local copies, waits for them, and re-layouts, on_device(): return (plain[0], plain[1], summed[0], summed[1])  1.54 us

profile of v2, /device:TPU:1, one launch (start us, length us, event | category | flops | bytes accessed | tf_op | source)
XLA Modules:
  0.0 74.4 jit_solution(3116039138945711787)
XLA Ops:
  0.6 32.8 %collect.1 = (bf16[2,32,2,24,128]{4,3,2,1,0:T(8,128)(2,1)S(1)}, bf16[2,32,2,24,128]{4,3,2,1,0:T(8,128)(2,1)S(1)}, bf16[32,2,24,128]{3,2,1,0:T(8,128)(2,1)S(1)}, bf16[2,24,128]{2,1,0:T(8,128)(2,1)S(1)}) custom-call(bf16[24,4096]{1,0:T(8,128)(2,1)} %q_ref.1, bf16[24,4096]{1,0:T(8,128)(2,1)} %k_ref.1, bf16[24,4096]{1,0:T(8,128)(2,1)} %v_ref.1, ...), custom_call_target="tpu_custom_call" | custom-call | tf_op jit(solution)/shard_map/collect/pallas_call | solution.py:189
  33.4 0.0 copy-start
  33.4 0.7 copy-done
  34.1 0.0 copy-start.1
  34.1 0.7 copy-done.1
  34.8 9.8 %one_head.1 = (bf16[32,24,128]{2,1,0:T(8,128)(2,1)S(1)}, f32[32,24,128]{2,1,0:T(8,128)S(1)}, f32[2,32,2,24,128]{4,3,2,1,0:T(8,128)S(1)}, bf16[2,32,2,24,128]{4,3,2,1,0:T(8,128)(2,1)S(1)}, bf16[2,24,128]{2,1,0:T(8,128)(2,1)S(1)}) custom-call(s32[12]{0:T(128)S(1)} %copy-done.1, bf16[2,32,2,24,128]{4,3,2,1,0:T(8,128)(2,1)S(1)} %get-tuple-element.15.refs_1_, ...), custom_call_target="tpu_custom_call" | custom-call | tf_op jit(solution)/shard_map/one_head/pallas_call | solution.py:381
  44.6 28.2 %spread.1 = (bf16[2,24,4096]{2,1,0:T(8,128)(2,1)S(1)}, bf16[2,2,24,4096]{3,2,1,0:T(8,128)(2,1)S(1)}) custom-call(bf16[32,24,128]{2,1,0:T(8,128)(2,1)S(1)} %get-tuple-element.19.att, f32[32,24,128]{2,1,0:T(8,128)S(1)} %get-tuple-element.20.dq, f32[2,32,2,24,128]{4,3,2,1,0:T(8,128)S(1)} %get-tuple-element.21.own, ...), custom_call_target="tpu_custom_call" | custom-call | tf_op jit(solution)/shard_map/spread/pallas_call | solution.py:492
  72.8 0.8 %slice_bitcast_fusion.2 = (bf16[24,4096]{1,0:T(8,128)(2,1)}, bf16[24,4096]{1,0:T(8,128)(2,1)}) fusion(bf16[2,24,4096]{2,1,0:T(8,128)(2,1)S(1)} %get-tuple-element.24), kind=kLoop, calls=%fused_computation.3 | loop fusion | bytes 786432 | tf_op jit(solution)/shard_map/squeeze | solution.py:517
  73.6 0.1 add_convert_fusion
  73.7 0.8 %slice_bitcast_fusion = (bf16[24,4096]{1,0:T(8,128)(2,1)}, bf16[24,4096]{1,0:T(8,128)(2,1)}) fusion(bf16[1,2,24,4096]{3,2,1,0:T(8,128)(2,1)S(1)} %add_convert_fusion), kind=kLoop, calls=%fused_computation.1 | loop fusion | bytes 786432 | tf_op jit(solution)/shard_map/squeeze | solution.py:517
Async XLA Ops:
  33.4 0.7 copy-start
  34.1 0.7 copy-start.1

commit v3 on v2

v3 whole, which is shorter than its diff:
```python
import functools

import jax
import jax.numpy as jnp
from jax import lax
from jax.experimental import pallas as pl
from jax.experimental.pallas import tpu as pltpu
from jax.sharding import Mesh
from jax.sharding import PartitionSpec as P

NAMES = ("z", "yl", "core", "x", "yh")
SIZES = (4, 2, 2, 4, 2)
D = 128
T = 3072
HEADS = 32
PIECE = 24
BLOCK = 384
PER_BLOCK = BLOCK // PIECE
OWN = 32
DOCS = 12
BQ = BLOCK
BK = 768
MASKED = -1.0e30
SCALE = D**-0.5
LOG2E = 1.4426950408889634
NT = (((1,), (1,)), ((), ()))
F32, BF16 = jnp.float32, jnp.bfloat16
MESH = pl.DeviceIdType.MESH


def dot(a, b):
    return jnp.dot(a, b, preferred_element_type=F32)


class Place:
    def __init__(self):
        self.z, self.yl, self.core, self.x, self.yh = (lax.axis_index(n) for n in NAMES)
        self.takes = lax.rem(self.z, 2)
        self.head = (self.x * 2 + self.yh) * 4 + self.z
        self.slot = self.z // 2 * PER_BLOCK + self.core * 8 + self.x * 2 + self.yh
        self.home = self.core == self.takes
        self.quarter = self.core * 2 + self.yl

    def owner_at(self, i, chip):
        k = lax.rem(i + self.head, HEADS)
        return k, dict(z=lax.rem(k, 4), yl=chip, core=self.takes, x=k // 8, yh=lax.rem(k // 4, 2))

    def token_at(self, i, side):
        s = lax.rem(i + self.slot, OWN)
        z = s // PER_BLOCK * 2 + self.core
        return s, dict(z=z, yl=lax.rem(self.yl + side, 2), core=lax.rem(s // 8, 2), x=lax.rem(s // 2, 4), yh=lax.rem(s, 2))

    def quarter_of(self, mine, side):
        return jnp.where(mine, self.core, 1 - self.core) * 2 + lax.rem(self.yl + side, 2)

    def other(self, yl, core):
        return dict(z=self.z, yl=yl, core=core, x=self.x, yh=self.yh)

    def sibling(self):
        return self.other(self.yl, 1 - self.core)

    def quarter_at(self, step):
        q = lax.rem(self.quarter + step + 4, 4)
        return self.other(lax.rem(q, 2), q // 2)


def signal(sem, device):
    pl.semaphore_signal(sem, 1, device_id=device, device_id_type=MESH)


def remote(src, dst, send, recv, device):
    return pltpu.make_async_remote_copy(src, dst, send, recv, device_id=device, device_id_type=MESH)


def drain(ref, sem):
    pltpu.make_async_copy(ref, ref, sem).wait()


def columns(head):
    return pl.ds(pl.multiple_of(head * D, D), D)


def settle(fewer, ref, part, sem):
    @pl.when(fewer)
    def _():
        drain(part, sem)

    @pl.when(jnp.logical_not(fewer))
    def _():
        drain(ref, sem)


def either(here, local, away):
    pl.when(here)(local)
    pl.when(jnp.logical_not(here))(away)


def most(ref):
    return ref.at[:, :, pl.ds(0, (HEADS - 1) * D)]


def starts_in(len_ref):
    starts = [jnp.int32(0)]
    for i in range(DOCS - 1):
        starts.append(starts[-1] + len_ref[i])
    return starts


def start_of(pos, starts):
    best = jnp.zeros_like(pos)
    for s in starts[1:]:
        best = jnp.where(pos >= s, s, best)
    return best


def base_of(quarter, i):
    return pl.multiple_of((quarter + 4 * i) * BLOCK, BLOCK)


def rows8(row):
    return pl.ds(pl.multiple_of(row, 8), PIECE)


def back(taps, hit1, hit2, src, row, token):
    out = taps[0] * src[rows8(row), :]
    out = out + taps[1] * (src[pl.ds(row + 1, PIECE), :] * hit1[pl.ds(token + 1, PIECE), :])
    return out + taps[2] * (src[pl.ds(row + 2, PIECE), :] * hit2[pl.ds(token + 2, PIECE), :])


def collect_kernel(
    q_ref, k_ref, v_ref, g_ref, all_taps, lengths,
    kc, vc, kt, vt, qc, go, gt, hit1, hit2, taps,
    xkv, ykv, xqg, xh, buf, stage, spare, size, load, ssem, rsem, lsem, psem, tsem,
):
    me = Place()
    loads = [pltpu.make_async_copy(src, buf.at[n], load.at[n]) for n, src in enumerate((k_ref, v_ref, q_ref, g_ref))]
    for copy in loads:
        copy.start()
    few = [
        pltpu.make_async_copy(all_taps.at[:, :, columns(me.z)], taps, load.at[4]),
        pltpu.make_async_copy(lengths, size, load.at[5]),
    ]
    for copy in few:
        copy.start()

    barrier = pltpu.get_barrier_semaphore()
    signal(barrier, me.sibling())
    signal(barrier, me.quarter_at(-1))
    signal(barrier, me.token_at(0, 1)[1])
    pl.when(jnp.logical_not(me.home))(lambda: signal(barrier, me.token_at(0, 0)[1]))

    def greet(i, _):
        for side in range(2):
            signal(barrier, me.token_at(i, side)[1])
        return 0

    lax.fori_loop(1, OWN, greet, 0)
    for copy in loads:
        copy.wait()
    either(
        me.home,
        lambda: pl.semaphore_wait(barrier, 2 * HEADS + 1),
        lambda: pl.semaphore_wait(barrier, 2 * HEADS + 2),
    )

    kv, qg = buf.at[pl.ds(0, 2)], buf.at[pl.ds(2, 2)]

    def side_at(chip):
        return jnp.where(me.yl == chip, 0, 1)

    def send_kv(i, chip):
        head, device = me.owner_at(i, chip)
        side = side_at(chip)
        remote(kv.at[:, :, columns(head)], xkv.at[side, me.slot], ssem.at[chip], rsem.at[side], device).start()

    def send_qg(i):
        head, device = me.owner_at(i, me.yl)
        remote(qg.at[:, :, columns(head)], xqg.at[me.slot], ssem.at[2], rsem.at[2], device).start()

    def keep_kv():
        return pltpu.make_async_copy(kv.at[:, :, columns(me.head)], xkv.at[0, me.slot], lsem.at[0])

    def keep_qg():
        return pltpu.make_async_copy(qg.at[:, :, columns(me.head)], xqg.at[me.slot], lsem.at[1])

    for chip in range(2):
        either(me.home & (me.yl == chip), lambda: keep_kv().start(), lambda: send_kv(0, chip))

    def all_kv(i, _):
        send_kv(i, 0)
        send_kv(i, 1)
        return 0

    lax.fori_loop(1, HEADS, all_kv, 0)
    either(me.home, lambda: keep_qg().start(), lambda: send_qg(0))

    def all_qg(i, _):
        send_qg(i)
        return 0

    lax.fori_loop(1, HEADS, all_qg, 0)

    swap = remote(xkv, ykv, psem.at[0], tsem.at[0], me.sibling())
    halos = [
        remote(xqg.at[i * PER_BLOCK + PER_BLOCK - 1, 0], xh.at[i], psem.at[1 + i], tsem.at[1 + i], me.quarter_at(1))
        for i in range(2)
    ]
    for copy in few:
        copy.wait()
    starts = starts_in(size)

    def hits(i, _):
        base = pl.multiple_of(i * 256, 256)
        pos = base + lax.broadcasted_iota(jnp.int32, (256, 1), 0)
        since = pos - start_of(pos, starts)
        hit1[pl.ds(base, 256), :] = jnp.broadcast_to(jnp.where(since >= 1, 1.0, 0.0).astype(F32), (256, D))
        hit2[pl.ds(base, 256), :] = jnp.broadcast_to(jnp.where(since >= 2, 1.0, 0.0).astype(F32), (256, D))
        return 0

    lax.fori_loop(0, T // 256, hits, 0)
    for ref in (hit1, hit2):
        ref[T:, :] = jnp.zeros((8, D), F32)
    for a in range(3):
        stage[a, 0:8, :] = jnp.zeros((8, D), F32)
    for ref in (kc, vc):
        ref[T:, :] = jnp.zeros((BK, D), BF16)
    for ref in (kt, vt):
        ref[:, T:] = jnp.zeros((D, BK), BF16)

    def unpack(ref, mine):
        def step(i, _):
            for side in range(2):
                base = base_of(me.quarter_of(mine, side), i)
                for j in range(PER_BLOCK):
                    for a in range(2):
                        stage[1 + a, rows8(base + j * PIECE + 8), :] = ref[side, i * PER_BLOCK + j, a].astype(F32)
            return 0

        lax.fori_loop(0, 2, step, 0)

    def mixed(a, base, rows):
        mix = taps[a, 0:1, :] * stage[a, pl.ds(base + 8, rows), :]
        mix = mix + taps[a, 1:2, :] * (stage[a, pl.ds(base + 7, rows), :] * hit1[pl.ds(base, rows), :])
        return mix + taps[a, 2:3, :] * (stage[a, pl.ds(base + 6, rows), :] * hit2[pl.ds(base, rows), :])

    settle(me.home, xkv.at[0], xkv.at[0, pl.ds(0, OWN - 1)], rsem.at[0])
    drain(xkv.at[1], rsem.at[1])
    pl.when(me.home)(lambda: keep_kv().wait())
    swap.start()
    unpack(xkv, True)
    swap.wait_recv()
    unpack(ykv, False)

    def keys(i, _):
        base = pl.multiple_of(i * 256, 256)
        for a, dst, dst_t in ((1, kc, kt), (2, vc, vt)):
            mix = mixed(a, base, 256)
            dst[pl.ds(base, 256), :] = mix.astype(BF16)
            dst_t[:, pl.ds(base, 256)] = mix.T.astype(BF16)
        return 0

    lax.fori_loop(0, T // 256, keys, 0)
    settle(me.home, xqg, xqg.at[pl.ds(0, OWN - 1)], rsem.at[2])
    pl.when(me.home)(lambda: keep_qg().wait())
    for copy in halos:
        copy.start()

    def queries(i, _):
        base = base_of(me.quarter, i)
        for j in range(PER_BLOCK):
            stage[0, rows8(base + j * PIECE + 8), :] = xqg[i * PER_BLOCK + j, 0].astype(F32)
            spare[j * PIECE : (j + 1) * PIECE, :] = xqg[i * PER_BLOCK + j, 1].astype(F32)
        g = spare[...]
        rows = pl.ds(pl.multiple_of(i * BLOCK, BLOCK), BLOCK)
        go[rows, :] = g.astype(BF16)
        gt[:, rows] = g.T
        return 0

    lax.fori_loop(0, 2, queries, 0)
    for copy in halos:
        copy.wait()
    before = lax.rem(me.quarter + 3, 4)
    for i in range(2):
        stage[0, rows8(base_of(before, i) + BLOCK - PIECE + 8), :] = xh[i].astype(F32)
    for i in range(2):
        qc[i * BLOCK : (i + 1) * BLOCK, :] = mixed(0, base_of(me.quarter, i), BLOCK).astype(BF16)
    for chip in range(2):
        settle(me.home & (me.yl == chip), kv, most(kv), ssem.at[chip])
    settle(me.home, qg, most(qg), ssem.at[2])
    swap.wait_send()


def collect(*arrays):
    vmem, hbm = pl.BlockSpec(memory_space=pltpu.VMEM), pl.BlockSpec(memory_space=pltpu.HBM)
    return pl.pallas_call(
        collect_kernel,
        out_shape=(
            pltpu.VMEM((T + BK, D), BF16), pltpu.VMEM((T + BK, D), BF16),
            pltpu.VMEM((D, T + BK), BF16), pltpu.VMEM((D, T + BK), BF16),
            pltpu.VMEM((2 * BLOCK, D), BF16), pltpu.VMEM((2 * BLOCK, D), BF16), pltpu.VMEM((D, 2 * BLOCK), F32),
            pltpu.VMEM((T + 8, D), F32), pltpu.VMEM((T + 8, D), F32),
            pltpu.VMEM((3, 3, D), F32),
        ),
        in_specs=[hbm] * 6,
        out_specs=(vmem,) * 10,
        scratch_shapes=[
            pltpu.VMEM((2, OWN, 2, PIECE, D), BF16),
            pltpu.VMEM((2, OWN, 2, PIECE, D), BF16),
            pltpu.VMEM((OWN, 2, PIECE, D), BF16),
            pltpu.VMEM((2, PIECE, D), BF16),
            pltpu.VMEM((4, PIECE, HEADS * D), BF16),
            pltpu.VMEM((3, T + 8, D), F32),
            pltpu.VMEM((BLOCK, D), F32),
            pltpu.SMEM((DOCS,), jnp.int32),
            pltpu.SemaphoreType.DMA((6,)),
            pltpu.SemaphoreType.DMA((3,)),
            pltpu.SemaphoreType.DMA((3,)),
            pltpu.SemaphoreType.DMA((2,)),
            pltpu.SemaphoreType.DMA((3,)),
            pltpu.SemaphoreType.DMA((3,)),
        ],
        compiler_params=pltpu.CompilerParams(collective_id=0, has_side_effects=True, vmem_limit_bytes=24 << 20),
        name="collect",
    )(*(pltpu.with_memory_space_constraint(x, pltpu.HBM) for x in arrays))


def head_kernel(lengths, kc, vc, kt, vt, qc, go, gt, att, dq, dk, dv, sc, size, sem):
    fetch = pltpu.make_async_copy(lengths, size, sem)
    fetch.start()
    quarter = lax.axis_index("core") * 2 + lax.axis_index("yl")
    for ref in (dk, dv):
        ref[...] = jnp.zeros(ref.shape, F32)
    for i in range(2):
        dq[i, 0:PIECE, :] = jnp.zeros((PIECE, D), F32)
        dq[i, PIECE + BLOCK :, :] = jnp.zeros((8, D), F32)
    fetch.wait()
    starts = starts_in(size)

    def queries(i, _):
        t0 = base_of(quarter, i)
        own = pl.ds(pl.multiple_of(i * BLOCK, BLOCK), BQ)
        q = qc[own, :]
        g = go[own, :]
        tpos = t0 + lax.broadcasted_iota(jnp.int32, (1, BQ), 1)
        tstart = start_of(tpos, starts)
        from_row = start_of(t0, starts) // D * D
        tiles = (t0 + BQ - from_row + BK - 1) // BK
        uio = lax.broadcasted_iota(jnp.int32, (BK, BQ), 0)

        def score(j, m):
            u0 = pl.multiple_of(from_row + j * BK, D)
            s = lax.dot_general(kc[pl.ds(u0, BK), :], q, NT, preferred_element_type=F32)
            s = jnp.where((uio <= tpos - u0) & (uio >= tstart - u0), s, MASKED)
            sc[pl.ds(u0, BK), :] = s
            return jnp.maximum(m, jnp.max(s, axis=0, keepdims=True))

        m = lax.fori_loop(0, tiles, score, jnp.full((1, BQ), MASKED, F32))
        shift = m * (SCALE * LOG2E)

        def weigh(j, carry):
            total, o = carry
            u0 = pl.multiple_of(from_row + j * BK, D)
            p = jnp.exp2(sc[pl.ds(u0, BK), :] * (SCALE * LOG2E) - shift)
            sc[pl.ds(u0, BK), :] = p
            total = total + jnp.sum(p, axis=0, keepdims=True)
            o = o + dot(vt[:, pl.ds(u0, BK)], p.astype(BF16))
            return total, o

        total, o = lax.fori_loop(0, tiles, weigh, (jnp.zeros((1, BQ), F32), jnp.zeros((D, BQ), F32)))
        inv = 1.0 / total
        o = o * inv
        delta = jnp.sum(gt[:, own] * o, axis=0, keepdims=True)
        att[own, :] = o.T

        def grads(j, acc):
            u0 = pl.multiple_of(from_row + j * BK, D)
            p = sc[pl.ds(u0, BK), :] * inv
            dp = lax.dot_general(vc[pl.ds(u0, BK), :], g, NT, preferred_element_type=F32)
            ds = (p * (dp - delta)).astype(BF16)
            dk[pl.ds(u0, BK), :] += dot(ds, q)
            dv[pl.ds(u0, BK), :] += dot(p.astype(BF16), g)
            return acc + dot(kt[:, pl.ds(u0, BK)], ds)

        acc = lax.fori_loop(0, tiles, grads, jnp.zeros((D, BQ), F32))
        dq[i, PIECE : PIECE + BLOCK, :] = acc.T
        return 0

    lax.fori_loop(0, 2, queries, 0)


def one_head(lengths, *arrays, kernel=head_kernel):
    vmem, hbm = pl.BlockSpec(memory_space=pltpu.VMEM), pl.BlockSpec(memory_space=pltpu.HBM)
    return pl.pallas_call(
        kernel,
        out_shape=(
            pltpu.VMEM((2 * BLOCK, D), F32),
            pltpu.VMEM((2, PIECE + BLOCK + 8, D), F32),
            pltpu.VMEM((T + BK, D), F32),
            pltpu.VMEM((T + BK, D), F32),
        ),
        in_specs=[hbm] + [vmem] * 7,
        out_specs=(vmem,) * 4,
        scratch_shapes=[pltpu.VMEM((T + BK, BQ), F32), pltpu.SMEM((DOCS,), jnp.int32), pltpu.SemaphoreType.DMA],
        compiler_params=pltpu.CompilerParams(vmem_limit_bytes=24 << 20),
        name="one_head",
    )(pltpu.with_memory_space_constraint(lengths, pltpu.HBM), *arrays)


def spread_kernel(
    att, dq, dk, dv, hit1, hit2, all_taps, out,
    buf_a, buf_k, other, edge, got, corner, ssem, rsem, lsem, psem, tsem,
):
    me = Place()
    out_a, out_k = out.at[2], out.at[pl.ds(0, 2)]
    barrier = pltpu.get_barrier_semaphore()
    signal(barrier, me.sibling())
    signal(barrier, me.quarter_at(1))
    for chip in range(2):
        @pl.when(jnp.logical_not(me.home & (me.yl == chip)))
        def _():
            signal(barrier, me.owner_at(0, chip)[1])

    def greet(i, _):
        for chip in range(2):
            signal(barrier, me.owner_at(i, chip)[1])
        return 0

    lax.fori_loop(1, HEADS, greet, 0)
    taps = [[all_taps[a, n : n + 1, :] * (SCALE if a < 2 else 1.0) for n in range(3)] for a in range(3)]

    def through(a, src, row, token):
        return back(taps[a], hit1, hit2, src, row, token)

    def keys_at(quarter, i, j):
        token = base_of(quarter, i) + j * PIECE
        return through(1, dk, token, token), through(2, dv, token, token)

    def rest(i, _):
        for side in range(2):
            for j in range(PER_BLOCK):
                grad_k, grad_v = keys_at(me.quarter_of(False, side), i, j)
                other[side, i * PER_BLOCK + j, 0] = grad_k.astype(BF16)
                other[side, i * PER_BLOCK + j, 1] = grad_v.astype(BF16)
        token = base_of(lax.rem(me.quarter + 3, 4), i) + BLOCK - PIECE
        after = jnp.minimum(i + jnp.where(me.quarter == 0, 1, 0), 1)
        edge[i] = through(0, dq.at[after], 0, token).astype(BF16)
        return 0

    lax.fori_loop(0, 2, rest, 0)
    either(
        me.home,
        lambda: pl.semaphore_wait(barrier, 2 * OWN + 1),
        lambda: pl.semaphore_wait(barrier, 2 * OWN + 2),
    )
    swap = remote(other, got, psem.at[0], tsem.at[0], me.sibling())
    turn = remote(edge, corner, psem.at[1], tsem.at[1], me.quarter_at(-1))
    swap.start()
    turn.start()
    mine = columns(me.head)

    def fill_a(i):
        s, _ = me.token_at(i, 0)
        block, j = s // PER_BLOCK, lax.rem(s, PER_BLOCK)
        buf_a[s, 0] = att[rows8(s * PIECE), :].astype(BF16)
        grad = through(0, dq.at[block], (j + 1) * PIECE, base_of(me.quarter, block) + j * PIECE)
        buf_a[s, 1] = (grad + jnp.where(j == PER_BLOCK - 1, corner[block].astype(F32), 0.0)).astype(BF16)

    def send_a(i):
        s, device = me.token_at(i, 0)
        remote(buf_a.at[s], out_a.at[:, :, mine], ssem.at[2], rsem.at[2], device).start()

    def keep_a():
        return pltpu.make_async_copy(buf_a.at[me.slot], out_a.at[:, :, mine], lsem.at[0])

    def fill_k(i):
        s, _ = me.token_at(i, 0)
        for side in range(2):
            grads = keys_at(me.quarter_of(True, side), s // PER_BLOCK, lax.rem(s, PER_BLOCK))
            for n, grad in enumerate(grads):
                buf_k[side, s, n] = (grad + got[side, s, n].astype(F32)).astype(BF16)

    def send_k(i, side):
        s, device = me.token_at(i, side)
        remote(buf_k.at[side, s], out_k.at[side, :, :, mine], ssem.at[side], rsem.at[side], device).start()

    def keep_k():
        return pltpu.make_async_copy(buf_k.at[0, me.slot], out_k.at[0, :, :, mine], lsem.at[1])

    turn.wait()
    fill_a(0)
    either(me.home, lambda: keep_a().start(), lambda: send_a(0))

    def all_a(i, _):
        fill_a(i)
        send_a(i)
        return 0

    lax.fori_loop(1, OWN, all_a, 0)
    swap.wait()
    fill_k(0)
    either(me.home, lambda: keep_k().start(), lambda: send_k(0, 0))
    send_k(0, 1)

    def all_k(i, _):
        fill_k(i)
        send_k(i, 0)
        send_k(i, 1)
        return 0

    lax.fori_loop(1, OWN, all_k, 0)
    for copy in (keep_a, keep_k):
        pl.when(me.home)(lambda: copy().wait())
    settle(me.home, out_a, most(out_a), rsem.at[2])
    settle(me.home, out_k.at[0], most(out_k.at[0]), rsem.at[0])
    drain(out_k.at[1], rsem.at[1])
    settle(me.home, buf_a, buf_a.at[pl.ds(0, OWN - 1)], ssem.at[2])
    settle(me.home, buf_k.at[0], buf_k.at[0, pl.ds(0, OWN - 1)], ssem.at[0])
    drain(buf_k.at[1], ssem.at[1])


def spread(*arrays):
    vmem = pl.BlockSpec(memory_space=pltpu.VMEM)
    return pl.pallas_call(
        spread_kernel,
        out_shape=pltpu.VMEM((3, 2, PIECE, HEADS * D), BF16),
        in_specs=[vmem] * 7,
        out_specs=pl.BlockSpec(memory_space=pl.ANY),
        scratch_shapes=[
            pltpu.VMEM((OWN, 2, PIECE, D), BF16),
            pltpu.VMEM((2, OWN, 2, PIECE, D), BF16),
            pltpu.VMEM((2, OWN, 2, PIECE, D), BF16),
            pltpu.VMEM((2, PIECE, D), BF16),
            pltpu.VMEM((2, OWN, 2, PIECE, D), BF16),
            pltpu.VMEM((2, PIECE, D), BF16),
            pltpu.SemaphoreType.DMA((3,)),
            pltpu.SemaphoreType.DMA((3,)),
            pltpu.SemaphoreType.DMA((2,)),
            pltpu.SemaphoreType.DMA((2,)),
            pltpu.SemaphoreType.DMA((2,)),
        ],
        compiler_params=pltpu.CompilerParams(collective_id=1, has_side_effects=True, vmem_limit_bytes=24 << 20),
        name="spread",
    )(*arrays)


def on_device(query_in, key_in, value_in, grad_out, kernel, lengths):
    *conv, hit1, hit2, taps = collect(query_in, key_in, value_in, grad_out, kernel, lengths)
    out = spread(*one_head(lengths, *conv), hit1, hit2, taps)
    summed = (out[0].astype(F32) + out[1].astype(F32)).astype(BF16)
    return out[2, 0], out[2, 1], summed[0], summed[1]


def solution(mesh):
    fine = Mesh(mesh.devices.reshape(SIZES), NAMES)
    rows = P(NAMES, None)
    return jax.shard_map(
        on_device,
        mesh=fine,
        in_specs=(rows, rows, rows, rows, P(None, None, ("x", "yh")), P()),
        out_specs=(rows,) * 4,
        check_vma=False,
    )
```

time: 74.6 us -> 67.9 us (0.910)
  Pallas kernels: 70.7 us -> 66.1 us
  local copies, waits for them, and re-layouts: 2.92 us -> 0.89 us
    pallas_call x3, Pallas kernels: 70.7 us -> 66.1 us  [the longest x1 31.7 us: collect(): pl.pallas_call(collect_kernel, out_shape=(pltpu.VMEM((T + BK, D), BF16),...]
    unnamed x4 -> x0, local copies, waits for them, and re-layouts: 1.39 us -> none
    squeeze x2 -> x1, local copies, waits for them, and re-layouts: 1.54 us -> 0.89 us  [on_device(): return (out[2, 0], out[2, 1], summed[0], summed[1])]
where the time goes in v3:
time: 67.9 us; the launch traced here: 67.7 us
  Pallas kernels  66.1 us (97%)
  local copies, waits for them, and re-layouts  0.89 us (1%)
    pallas_call x1, Pallas kernels, collect(): pl.pallas_call(collect_kernel, out_shape=(pltpu.VMEM((T + BK, D), BF16),...  31.7 us
    pallas_call x1, Pallas kernels, spread(): pl.pallas_call(spread_kernel, out_shape=pltpu.VMEM((3, 2, PIECE, HEADS *...  26.4 us
    pallas_call x1, Pallas kernels, one_head(): pl.pallas_call(kernel, out_shape=(pltpu.VMEM((2 * BLOCK, D), F32), pltpu....  7.95 us

profile of v3, /device:TPU:1, one launch (start us, length us, event | category | flops | bytes accessed | tf_op | source)
XLA Modules:
  0.0 67.7 jit_solution(9482278660734846401)
XLA Ops:
  0.6 31.7 %collect.1 = (bf16[3840,128]{1,0:T(8,128)(2,1)S(1)}, bf16[3840,128]{1,0:T(8,128)(2,1)S(1)}, bf16[128,3840]{1,0:T(8,128)(2,1)S(1)}, bf16[128,3840]{1,0:T(8,128)(2...) custom-call(bf16[24,4096]{1,0:T(8,128)(2,1)} %q_ref.1, ...), custom_call_target="tpu_custom_call" | custom-call | tf_op jit(solution)/shard_map/collect/pallas_call | solution.py:295
  32.4 8.0 %one_head.1 = (f32[768,128]{1,0:T(8,128)S(1)}, f32[2,416,128]{2,1,0:T(8,128)S(1)}, f32[3840,128]{1,0:T(8,128)S(1)}, f32[3840,128]{1,0:T(8,128)S(1)}) custom-call(s32[12]{0:T(128)} %lengths.3, bf16[3840,128]{1,0:T(8,128)(2,1)S(1)} %get-tuple-element.18.kc, bf16[3840,128]{1,0:T(8,128)(2,1)S(1)} %get-tuple-element.19.vc, ...), custom_call_target="tpu_custom_call" | custom-call | tf_op jit(solution)/shard_map/one_head/pallas_call | solution.py:393
  40.3 26.4 %spread.1 = bf16[3,2,24,4096]{3,2,1,0:T(8,128)(2,1)S(1)} custom-call(f32[768,128]{1,0:T(8,128)S(1)} %get-tuple-element.25.att, f32[2,416,128]{2,1,0:T(8,128)S(1)} %get-tuple-element.26.dq, f32[3840,128]{1,0:T(8,128)S(1)} %get-tuple-element.27.dk, f32[3840,128]{1,0:T(8,128)S(1)} %get-tuple-element.28.dv, f32[3080,128]{1,0:T(8,128)S(1)} %get-tuple-element.29.hit1, ...), custom_call_target="tpu_custom_call" | custom-call | tf_op jit(solution)/shard_map/spread/pallas_call | solution.py:523
  66.8 0.1 add_convert_fusion
  66.9 0.9 %slice_bitcast_fusion = (bf16[24,4096]{1,0:T(8,128)(2,1)}, bf16[24,4096]{1,0:T(8,128)(2,1)}, bf16[24,4096]{1,0:T(8,128)(2,1)}, bf16[24,4096]{1,0:T(8,128)(2,1)}) fusion(bf16[1,2,24,4096]{3,2,1,0:T(8,128)(2,1)S(1)} %add_convert_fusion, bf16[3,2,24,4096]{3,2,1,0:T(8,128)(2,1)S(1)} %spread.1), kind=kLoop, calls=%fused_computation.1 | loop fusion | bytes 1572864 | tf_op jit(solution)/shard_map/squeeze | solution.py:550

commit v4 on v3

--- a/solution.py
+++ b/solution.py
@@ -40,6 +40,7 @@
         self.slot = self.z // 2 * PER_BLOCK + self.core * 8 + self.x * 2 + self.yh
         self.home = self.core == self.takes
         self.quarter = self.core * 2 + self.yl
+        self.last = (self.core == 1) & (self.x == 3) & (self.yh == 1)
 
     def owner_at(self, i, chip):
         k = lax.rem(i + self.head, HEADS)
@@ -62,6 +63,15 @@
     def quarter_at(self, step):
         q = lax.rem(self.quarter + step + 4, 4)
         return self.other(lax.rem(q, 2), q // 2)
+
+    def follower_at(self, i):
+        k, device = self.owner_at(i, 0)
+        q = lax.rem(self.takes * 2 + self.yl + 1, 4)
+        return k, {**device, "yl": lax.rem(q, 2), "core": q // 2}
+
+    def leader(self, i):
+        q = lax.rem(self.quarter + 3, 4)
+        return dict(z=q // 2 + 2 * i, yl=lax.rem(q, 2), core=1, x=3, yh=1)
 
 
 def signal(sem, device):
@@ -145,7 +155,8 @@
 
     barrier = pltpu.get_barrier_semaphore()
     signal(barrier, me.sibling())
-    signal(barrier, me.quarter_at(-1))
+    for i in range(2):
+        signal(barrier, me.leader(i))
     signal(barrier, me.token_at(0, 1)[1])
     pl.when(jnp.logical_not(me.home))(lambda: signal(barrier, me.token_at(0, 0)[1]))
 
@@ -157,41 +168,50 @@
     lax.fori_loop(1, OWN, greet, 0)
     for copy in loads:
         copy.wait()
-    either(
-        me.home,
-        lambda: pl.semaphore_wait(barrier, 2 * HEADS + 1),
-        lambda: pl.semaphore_wait(barrier, 2 * HEADS + 2),
-    )
-
-    kv, qg = buf.at[pl.ds(0, 2)], buf.at[pl.ds(2, 2)]
+    greeted = 2 * HEADS + 1 - jnp.where(me.home, 1, 0) + jnp.where(me.last, HEADS, 0)
+    pl.semaphore_wait(barrier, greeted)
+
+    qg = buf.at[pl.ds(2, 2)]
 
     def side_at(chip):
         return jnp.where(me.yl == chip, 0, 1)
 
-    def send_kv(i, chip):
+    def send_kv(n, i, chip):
         head, device = me.owner_at(i, chip)
         side = side_at(chip)
-        remote(kv.at[:, :, columns(head)], xkv.at[side, me.slot], ssem.at[chip], rsem.at[side], device).start()
+        remote(buf.at[n, :, columns(head)], xkv.at[n, side, me.slot], ssem.at[2 * n + chip], rsem.at[2 * n + side], device).start()
 
     def send_qg(i):
         head, device = me.owner_at(i, me.yl)
-        remote(qg.at[:, :, columns(head)], xqg.at[me.slot], ssem.at[2], rsem.at[2], device).start()
-
-    def keep_kv():
-        return pltpu.make_async_copy(kv.at[:, :, columns(me.head)], xkv.at[0, me.slot], lsem.at[0])
+        remote(qg.at[:, :, columns(head)], xqg.at[me.slot], ssem.at[4], rsem.at[4], device).start()
+
+    def keep_kv(n):
+        return pltpu.make_async_copy(buf.at[n, :, columns(me.head)], xkv.at[n, 0, me.slot], lsem.at[n])
 
     def keep_qg():
-        return pltpu.make_async_copy(qg.at[:, :, columns(me.head)], xqg.at[me.slot], lsem.at[1])
-
-    for chip in range(2):
-        either(me.home & (me.yl == chip), lambda: keep_kv().start(), lambda: send_kv(0, chip))
-
-    def all_kv(i, _):
-        send_kv(i, 0)
-        send_kv(i, 1)
-        return 0
-
-    lax.fori_loop(1, HEADS, all_kv, 0)
+        return pltpu.make_async_copy(qg.at[:, :, columns(me.head)], xqg.at[me.slot], lsem.at[2])
+
+    for n in range(2):
+        for chip in range(2):
+            either(me.home & (me.yl == chip), lambda: keep_kv(n).start(), lambda: send_kv(n, 0, chip))
+
+        def all_kv(i, _, n=n):
+            send_kv(n, i, 0)
+            send_kv(n, i, 1)
+            return 0
+
+        lax.fori_loop(1, HEADS, all_kv, 0)
+
+    @pl.when(me.last)
+    def _():
+        def lead(i, _):
+            head, device = me.follower_at(i)
+            i = me.z // 2
+            remote(buf.at[2, :, columns(head)], xh.at[i], ssem.at[5], tsem.at[i], device).start()
+            return 0
+
+        lax.fori_loop(0, HEADS, lead, 0)
+
     either(me.home, lambda: keep_qg().start(), lambda: send_qg(0))
 
     def all_qg(i, _):
@@ -200,11 +220,7 @@
 
     lax.fori_loop(1, HEADS, all_qg, 0)
 
-    swap = remote(xkv, ykv, psem.at[0], tsem.at[0], me.sibling())
-    halos = [
-        remote(xqg.at[i * PER_BLOCK + PER_BLOCK - 1, 0], xh.at[i], psem.at[1 + i], tsem.at[1 + i], me.quarter_at(1))
-        for i in range(2)
-    ]
+    swaps = [remote(xkv.at[n], ykv.at[n], psem.at[n], tsem.at[2 + n], me.sibling()) for n in range(2)]
     for copy in few:
         copy.wait()
     starts = starts_in(size)
@@ -227,13 +243,12 @@
     for ref in (kt, vt):
         ref[:, T:] = jnp.zeros((D, BK), BF16)
 
-    def unpack(ref, mine):
+    def unpack(n, ref, mine):
         def step(i, _):
             for side in range(2):
                 base = base_of(me.quarter_of(mine, side), i)
                 for j in range(PER_BLOCK):
-                    for a in range(2):
-                        stage[1 + a, rows8(base + j * PIECE + 8), :] = ref[side, i * PER_BLOCK + j, a].astype(F32)
+                    stage[1 + n, rows8(base + j * PIECE + 8), :] = ref[n, side, i * PER_BLOCK + j].astype(F32)
             return 0
 
         lax.fori_loop(0, 2, step, 0)
@@ -243,27 +258,25 @@
         mix = mix + taps[a, 1:2, :] * (stage[a, pl.ds(base + 7, rows), :] * hit1[pl.ds(base, rows), :])
         return mix + taps[a, 2:3, :] * (stage[a, pl.ds(base + 6, rows), :] * hit2[pl.ds(base, rows), :])
 
-    settle(me.home, xkv.at[0], xkv.at[0, pl.ds(0, OWN - 1)], rsem.at[0])
-    drain(xkv.at[1], rsem.at[1])
-    pl.when(me.home)(lambda: keep_kv().wait())
-    swap.start()
-    unpack(xkv, True)
-    swap.wait_recv()
-    unpack(ykv, False)
-
-    def keys(i, _):
-        base = pl.multiple_of(i * 256, 256)
-        for a, dst, dst_t in ((1, kc, kt), (2, vc, vt)):
-            mix = mixed(a, base, 256)
+    for n, (dst, dst_t) in enumerate(((kc, kt), (vc, vt))):
+        settle(me.home, xkv.at[n, 0], xkv.at[n, 0, pl.ds(0, OWN - 1)], rsem.at[2 * n])
+        drain(xkv.at[n, 1], rsem.at[2 * n + 1])
+        pl.when(me.home)(lambda: keep_kv(n).wait())
+        swaps[n].start()
+        unpack(n, xkv, True)
+        swaps[n].wait_recv()
+        unpack(n, ykv, False)
+
+        def keys(i, _, n=n, dst=dst, dst_t=dst_t):
+            base = pl.multiple_of(i * 256, 256)
+            mix = mixed(1 + n, base, 256)
             dst[pl.ds(base, 256), :] = mix.astype(BF16)
             dst_t[:, pl.ds(base, 256)] = mix.T.astype(BF16)
-        return 0
-
-    lax.fori_loop(0, T // 256, keys, 0)
-    settle(me.home, xqg, xqg.at[pl.ds(0, OWN - 1)], rsem.at[2])
+            return 0
+
+        lax.fori_loop(0, T // 256, keys, 0)
+    settle(me.home, xqg, xqg.at[pl.ds(0, OWN - 1)], rsem.at[4])
     pl.when(me.home)(lambda: keep_qg().wait())
-    for copy in halos:
-        copy.start()
 
     def queries(i, _):
         base = base_of(me.quarter, i)
@@ -277,17 +290,19 @@
         return 0
 
     lax.fori_loop(0, 2, queries, 0)
-    for copy in halos:
-        copy.wait()
     before = lax.rem(me.quarter + 3, 4)
     for i in range(2):
+        drain(xh.at[i], tsem.at[i])
         stage[0, rows8(base_of(before, i) + BLOCK - PIECE + 8), :] = xh[i].astype(F32)
     for i in range(2):
         qc[i * BLOCK : (i + 1) * BLOCK, :] = mixed(0, base_of(me.quarter, i), BLOCK).astype(BF16)
-    for chip in range(2):
-        settle(me.home & (me.yl == chip), kv, most(kv), ssem.at[chip])
-    settle(me.home, qg, most(qg), ssem.at[2])
-    swap.wait_send()
+    for n in range(2):
+        for chip in range(2):
+            fewer = buf.at[n, :, pl.ds(0, (HEADS - 1) * D)]
+            settle(me.home & (me.yl == chip), buf.at[n], fewer, ssem.at[2 * n + chip])
+        swaps[n].wait_send()
+    settle(me.home, qg, most(qg), ssem.at[4])
+    pl.when(me.last)(lambda: drain(buf.at[2], ssem.at[5]))
 
 
 def collect(*arrays):
@@ -304,8 +319,8 @@
         in_specs=[hbm] * 6,
         out_specs=(vmem,) * 10,
         scratch_shapes=[
-            pltpu.VMEM((2, OWN, 2, PIECE, D), BF16),
-            pltpu.VMEM((2, OWN, 2, PIECE, D), BF16),
+            pltpu.VMEM((2, 2, OWN, PIECE, D), BF16),
+            pltpu.VMEM((2, 2, OWN, PIECE, D), BF16),
             pltpu.VMEM((OWN, 2, PIECE, D), BF16),
             pltpu.VMEM((2, PIECE, D), BF16),
             pltpu.VMEM((4, PIECE, HEADS * D), BF16),
@@ -313,11 +328,11 @@
             pltpu.VMEM((BLOCK, D), F32),
             pltpu.SMEM((DOCS,), jnp.int32),
             pltpu.SemaphoreType.DMA((6,)),
-            pltpu.SemaphoreType.DMA((3,)),
+            pltpu.SemaphoreType.DMA((6,)),
+            pltpu.SemaphoreType.DMA((5,)),
             pltpu.SemaphoreType.DMA((3,)),
             pltpu.SemaphoreType.DMA((2,)),
-            pltpu.SemaphoreType.DMA((3,)),
-            pltpu.SemaphoreType.DMA((3,)),
+            pltpu.SemaphoreType.DMA((4,)),
         ],
         compiler_params=pltpu.CompilerParams(collective_id=0, has_side_effects=True, vmem_limit_bytes=24 << 20),
         name="collect",
@@ -458,12 +473,14 @@
     turn.start()
     mine = columns(me.head)
 
-    def fill_a(i):
+    def fill_a(i, edges):
         s, _ = me.token_at(i, 0)
         block, j = s // PER_BLOCK, lax.rem(s, PER_BLOCK)
         buf_a[s, 0] = att[rows8(s * PIECE), :].astype(BF16)
         grad = through(0, dq.at[block], (j + 1) * PIECE, base_of(me.quarter, block) + j * PIECE)
-        buf_a[s, 1] = (grad + jnp.where(j == PER_BLOCK - 1, corner[block].astype(F32), 0.0)).astype(BF16)
+        if edges:
+            grad = grad + corner[block].astype(F32)
+        buf_a[s, 1] = grad.astype(BF16)
 
     def send_a(i):
         s, device = me.token_at(i, 0)
@@ -486,16 +503,22 @@
     def keep_k():
         return pltpu.make_async_copy(buf_k.at[0, me.slot], out_k.at[0, :, :, mine], lsem.at[1])
 
+    def all_a(edges):
+        def step(i, _):
+            s, _ = me.token_at(i, 0)
+
+            @pl.when((lax.rem(s, PER_BLOCK) == PER_BLOCK - 1) == edges)
+            def _():
+                fill_a(i, edges)
+                either(me.home & (i == 0), lambda: keep_a().start(), lambda: send_a(i))
+
+            return 0
+
+        lax.fori_loop(0, OWN, step, 0)
+
+    all_a(False)
     turn.wait()
-    fill_a(0)
-    either(me.home, lambda: keep_a().start(), lambda: send_a(0))
-
-    def all_a(i, _):
-        fill_a(i)
-        send_a(i)
-        return 0
-
-    lax.fori_loop(1, OWN, all_a, 0)
+    all_a(True)
     swap.wait()
     fill_k(0)
     either(me.home, lambda: keep_k().start(), lambda: send_k(0, 0))

time: 67.9 us -> 63.3 us (0.932)
  Pallas kernels: 66.1 us -> 61.5 us
    pallas_call x1, Pallas kernels: 26.4 us -> 23 us  [spread(): pl.pallas_call(spread_kernel, out_shape=pltpu.VMEM((3, 2, PIECE, HEADS *...]
    pallas_call x1, Pallas kernels: 31.7 us -> 30.6 us  [collect(): pl.pallas_call(collect_kernel, out_shape=(pltpu.VMEM((T + BK, D), BF16),...]
where the time goes in v4:
time: 63.3 us; the launch traced here: 63.1 us
  Pallas kernels  61.5 us (97%)
  local copies, waits for them, and re-layouts  0.89 us (1%)
  between operations  0.66 us (1%)
    pallas_call x1, Pallas kernels, collect(): pl.pallas_call(collect_kernel, out_shape=(pltpu.VMEM((T + BK, D), BF16),...  30.6 us
    pallas_call x1, Pallas kernels, spread(): pl.pallas_call(spread_kernel, out_shape=pltpu.VMEM((3, 2, PIECE, HEADS *...  23 us
    pallas_call x1, Pallas kernels, one_head(): pl.pallas_call(kernel, out_shape=(pltpu.VMEM((2 * BLOCK, D), F32), pltpu....  7.92 us

profile of v4, /device:TPU:1, one launch (start us, length us, event | category | flops | bytes accessed | tf_op | source)
XLA Modules:
  0.0 63.1 jit_solution(6707651320285868679)
XLA Ops:
  0.6 30.6 %collect.1 = (bf16[3840,128]{1,0:T(8,128)(2,1)S(1)}, bf16[3840,128]{1,0:T(8,128)(2,1)S(1)}, bf16[128,3840]{1,0:T(8,128)(2,1)S(1)}, bf16[128,3840]{1,0:T(8,128)(2...) custom-call(bf16[24,4096]{1,0:T(8,128)(2,1)} %q_ref.1, ...), custom_call_target="tpu_custom_call" | custom-call | tf_op jit(solution)/shard_map/collect/pallas_call | solution.py:310
  31.2 7.9 %one_head.1 = (f32[768,128]{1,0:T(8,128)S(1)}, f32[2,416,128]{2,1,0:T(8,128)S(1)}, f32[3840,128]{1,0:T(8,128)S(1)}, f32[3840,128]{1,0:T(8,128)S(1)}) custom-call(s32[12]{0:T(128)} %lengths.3, bf16[3840,128]{1,0:T(8,128)(2,1)S(1)} %get-tuple-element.18.kc, bf16[3840,128]{1,0:T(8,128)(2,1)S(1)} %get-tuple-element.19.vc, ...), custom_call_target="tpu_custom_call" | custom-call | tf_op jit(solution)/shard_map/one_head/pallas_call | solution.py:408
  39.1 23.0 %spread.1 = bf16[3,2,24,4096]{3,2,1,0:T(8,128)(2,1)S(1)} custom-call(f32[768,128]{1,0:T(8,128)S(1)} %get-tuple-element.25.att, f32[2,416,128]{2,1,0:T(8,128)S(1)} %get-tuple-element.26.dq, f32[3840,128]{1,0:T(8,128)S(1)} %get-tuple-element.27.dk, f32[3840,128]{1,0:T(8,128)S(1)} %get-tuple-element.28.dv, f32[3080,128]{1,0:T(8,128)S(1)} %get-tuple-element.29.hit1, ...), custom_call_target="tpu_custom_call" | custom-call | tf_op jit(solution)/shard_map/spread/pallas_call | solution.py:546
  62.1 0.1 add_convert_fusion
  62.2 0.9 %slice_bitcast_fusion = (bf16[24,4096]{1,0:T(8,128)(2,1)}, bf16[24,4096]{1,0:T(8,128)(2,1)}, bf16[24,4096]{1,0:T(8,128)(2,1)}, bf16[24,4096]{1,0:T(8,128)(2,1)}) fusion(bf16[1,2,24,4096]{3,2,1,0:T(8,128)(2,1)S(1)} %add_convert_fusion, bf16[3,2,24,4096]{3,2,1,0:T(8,128)(2,1)S(1)} %spread.1), kind=kLoop, calls=%fused_computation.1 | loop fusion | bytes 1572864 | tf_op jit(solution)/shard_map/squeeze | solution.py:573

commit v5 on v4

v5 whole, which is shorter than its diff:
```python
import functools

import jax
import jax.numpy as jnp
from jax import lax
from jax.experimental import pallas as pl
from jax.experimental.pallas import tpu as pltpu
from jax.sharding import Mesh
from jax.sharding import PartitionSpec as P

NAMES = ("z", "yl", "core", "x", "yh")
SIZES = (4, 2, 2, 4, 2)
D = 128
T = 3072
HEADS = 32
PIECE = 24
BLOCK = 384
PER_BLOCK = BLOCK // PIECE
OWN = 32
DOCS = 12
BQ = BLOCK
BK = 768
LONGEST = 1920
MASKED = -1.0e30
SCALE = D**-0.5
LOG2E = 1.4426950408889634
NT = (((1,), (1,)), ((), ()))
F32, BF16 = jnp.float32, jnp.bfloat16
MESH = pl.DeviceIdType.MESH


def dot(a, b):
    return jnp.dot(a, b, preferred_element_type=F32)


class Place:
    def __init__(self):
        self.z, self.yl, self.core, self.x, self.yh = (lax.axis_index(n) for n in NAMES)
        self.takes = lax.rem(self.z, 2)
        self.head = (self.x * 2 + self.yh) * 4 + self.z
        self.slot = self.z // 2 * PER_BLOCK + self.core * 8 + self.x * 2 + self.yh
        self.home = self.core == self.takes
        self.quarter = self.core * 2 + self.yl
        self.last = (self.core == 1) & (self.x == 3) & (self.yh == 1)

    def owner_at(self, i, chip):
        k = lax.rem(i + self.head, HEADS)
        return k, dict(z=lax.rem(k, 4), yl=chip, core=self.takes, x=k // 8, yh=lax.rem(k // 4, 2))

    def token_at(self, i, side):
        s = lax.rem(i + self.slot, OWN)
        z = s // PER_BLOCK * 2 + self.core
        return s, dict(z=z, yl=lax.rem(self.yl + side, 2), core=lax.rem(s // 8, 2), x=lax.rem(s // 2, 4), yh=lax.rem(s, 2))

    def quarter_of(self, mine, side):
        return jnp.where(mine, self.core, 1 - self.core) * 2 + lax.rem(self.yl + side, 2)

    def other(self, yl, core):
        return dict(z=self.z, yl=yl, core=core, x=self.x, yh=self.yh)

    def sibling(self):
        return self.other(self.yl, 1 - self.core)

    def quarter_at(self, step):
        q = lax.rem(self.quarter + step + 4, 4)
        return self.other(lax.rem(q, 2), q // 2)

    def follower_at(self, i):
        k, device = self.owner_at(i, 0)
        q = lax.rem(self.takes * 2 + self.yl + 1, 4)
        return k, {**device, "yl": lax.rem(q, 2), "core": q // 2}

    def leader(self, i):
        q = lax.rem(self.quarter + 3, 4)
        return dict(z=q // 2 + 2 * i, yl=lax.rem(q, 2), core=1, x=3, yh=1)


def signal(sem, device):
    pl.semaphore_signal(sem, 1, device_id=device, device_id_type=MESH)


def remote(src, dst, send, recv, device):
    return pltpu.make_async_remote_copy(src, dst, send, recv, device_id=device, device_id_type=MESH)


def drain(ref, sem):
    pltpu.make_async_copy(ref, ref, sem).wait()


def columns(head):
    return pl.ds(pl.multiple_of(head * D, D), D)


def settle(fewer, ref, part, sem):
    @pl.when(fewer)
    def _():
        drain(part, sem)

    @pl.when(jnp.logical_not(fewer))
    def _():
        drain(ref, sem)


def either(here, local, away):
    pl.when(here)(local)
    pl.when(jnp.logical_not(here))(away)


def most(ref):
    return ref.at[:, pl.ds(0, (HEADS - 1) * D)]


def starts_in(len_ref):
    starts = [jnp.int32(0)]
    for i in range(DOCS - 1):
        starts.append(starts[-1] + len_ref[i])
    return starts


def start_of(pos, starts):
    best = jnp.zeros_like(pos)
    for s in starts[1:]:
        best = jnp.where(pos >= s, s, best)
    return best


def base_of(quarter, i):
    return pl.multiple_of((quarter + 4 * i) * BLOCK, BLOCK)


def rows8(row):
    return pl.ds(pl.multiple_of(row, 8), PIECE)


def back(taps, hit1, hit2, src, row, token):
    out = taps[0] * src[rows8(row), :]
    out = out + taps[1] * (src[pl.ds(row + 1, PIECE), :] * hit1[pl.ds(token + 1, PIECE), :])
    return out + taps[2] * (src[pl.ds(row + 2, PIECE), :] * hit2[pl.ds(token + 2, PIECE), :])


KEY, VALUE, QUERY, GRAD = range(4)


def kernel_body(
    q_ref, k_ref, v_ref, g_ref, all_taps, lengths, out,
    buf, xkv, ykv, xqg, xh, stage, spare, hit1, hit2, taps, size,
    kc, vc, kt, vt, qc, go, gt, sc, peak, whole, heads_out, dq, dk, dv,
    buf_a, buf_k, other, edge, got, corner,
    load, ssem, rsem, lsem, psem, tsem,
    ssem2, rsem2, lsem2, psem2, tsem2,
):
    me = Place()
    loads = [pltpu.make_async_copy(src, buf.at[n], load.at[n]) for n, src in enumerate((k_ref, v_ref, q_ref, g_ref))]
    for copy in loads:
        copy.start()
    few = [
        pltpu.make_async_copy(all_taps.at[:, :, columns(me.z)], taps, load.at[4]),
        pltpu.make_async_copy(lengths, size, load.at[5]),
    ]
    for copy in few:
        copy.start()

    barrier = pltpu.get_barrier_semaphore()
    signal(barrier, me.sibling())
    signal(barrier, me.quarter_at(1))
    for i in range(2):
        signal(barrier, me.leader(i))
    signal(barrier, me.token_at(0, 1)[1])
    pl.when(jnp.logical_not(me.home))(lambda: signal(barrier, me.token_at(0, 0)[1]))

    def greet(i, _):
        for side in range(2):
            signal(barrier, me.token_at(i, side)[1])
        return 0

    lax.fori_loop(1, OWN, greet, 0)
    for copy in loads:
        copy.wait()
    greeted = 2 * HEADS + 2 - jnp.where(me.home, 1, 0) + jnp.where(me.last, HEADS, 0)
    pl.semaphore_wait(barrier, greeted)

    def send_kv(n, i, chip):
        head, device = me.owner_at(i, chip)
        side = jnp.where(me.yl == chip, 0, 1)
        remote(buf.at[n, :, columns(head)], xkv.at[n, side, me.slot], ssem.at[2 * n + chip], rsem.at[2 * n + side], device).start()

    def keep_kv(n):
        return pltpu.make_async_copy(buf.at[n, :, columns(me.head)], xkv.at[n, 0, me.slot], lsem.at[n])

    def send_qg(n, i):
        head, device = me.owner_at(i, me.yl)
        remote(buf.at[n, :, columns(head)], xqg.at[n - 2, me.slot], ssem.at[2 + n], rsem.at[2 + n], device).start()

    def keep_qg(n):
        return pltpu.make_async_copy(buf.at[n, :, columns(me.head)], xqg.at[n - 2, me.slot], lsem.at[n])

    for n in (KEY, QUERY, VALUE, GRAD):
        if n < 2:
            for chip in range(2):
                either(me.home & (me.yl == chip), lambda: keep_kv(n).start(), lambda: send_kv(n, 0, chip))

            def all_kv(i, _, n=n):
                send_kv(n, i, 0)
                send_kv(n, i, 1)
                return 0

            lax.fori_loop(1, HEADS, all_kv, 0)
        else:
            either(me.home, lambda: keep_qg(n).start(), lambda: send_qg(n, 0))

            def all_qg(i, _, n=n):
                send_qg(n, i)
                return 0

            lax.fori_loop(1, HEADS, all_qg, 0)
        if n == QUERY:
            @pl.when(me.last)
            def _():
                def lead(i, _):
                    head, device = me.follower_at(i)
                    block = me.z // 2
                    remote(buf.at[QUERY, :, columns(head)], xh.at[block], ssem.at[6], tsem.at[block], device).start()
                    return 0

                lax.fori_loop(0, HEADS, lead, 0)

    swaps = [remote(xkv.at[n], ykv.at[n], psem.at[n], tsem.at[2 + n], me.sibling()) for n in range(2)]
    for copy in few:
        copy.wait()
    starts = starts_in(size)

    def hits(i, _):
        base = pl.multiple_of(i * 256, 256)
        pos = base + lax.broadcasted_iota(jnp.int32, (256, 1), 0)
        since = pos - start_of(pos, starts)
        hit1[pl.ds(base, 256), :] = jnp.broadcast_to(jnp.where(since >= 1, 1.0, 0.0).astype(F32), (256, D))
        hit2[pl.ds(base, 256), :] = jnp.broadcast_to(jnp.where(since >= 2, 1.0, 0.0).astype(F32), (256, D))
        return 0

    lax.fori_loop(0, T // 256, hits, 0)
    for ref in (hit1, hit2):
        ref[T:, :] = jnp.zeros((8, D), F32)
    for a in range(3):
        stage[a, 0:8, :] = jnp.zeros((8, D), F32)
    for ref in (dk, dv):
        ref[...] = jnp.zeros(ref.shape, F32)
    for i in range(2):
        dq[i, 0:PIECE, :] = jnp.zeros((PIECE, D), F32)
        dq[i, PIECE + BLOCK :, :] = jnp.zeros((8, D), F32)

    def unpack(n, ref, mine):
        def step(i, _):
            for side in range(2):
                base = base_of(me.quarter_of(mine, side), i)
                for j in range(PER_BLOCK):
                    stage[1 + n, rows8(base + j * PIECE + 8), :] = ref[n, side, i * PER_BLOCK + j].astype(F32)
            return 0

        lax.fori_loop(0, 2, step, 0)

    def mixed(a, base, rows):
        mix = taps[a, 0:1, :] * stage[a, pl.ds(base + 8, rows), :]
        mix = mix + taps[a, 1:2, :] * (stage[a, pl.ds(base + 7, rows), :] * hit1[pl.ds(base, rows), :])
        return mix + taps[a, 2:3, :] * (stage[a, pl.ds(base + 6, rows), :] * hit2[pl.ds(base, rows), :])

    def arrive_kv(n):
        settle(me.home, xkv.at[n, 0], xkv.at[n, 0, pl.ds(0, OWN - 1)], rsem.at[2 * n])
        drain(xkv.at[n, 1], rsem.at[2 * n + 1])
        pl.when(me.home)(lambda: keep_kv(n).wait())
        swaps[n].start()

    def convolve_kv(n, dst, dst_t):
        unpack(n, xkv, True)
        swaps[n].wait_recv()
        unpack(n, ykv, False)

        def step(i, _):
            base = pl.multiple_of(i * 256, 256)
            mix = mixed(1 + n, base, 256)
            dst[pl.ds(base, 256), :] = mix.astype(BF16)
            dst_t[:, pl.ds(base, 256)] = mix.T.astype(BF16)
            return 0

        lax.fori_loop(0, T // 256, step, 0)

    def arrive_qg(n):
        settle(me.home, xqg.at[n - 2], xqg.at[n - 2, pl.ds(0, OWN - 1)], rsem.at[2 + n])
        pl.when(me.home)(lambda: keep_qg(n).wait())

    arrive_kv(KEY)
    convolve_kv(KEY, kc, kt)
    arrive_qg(QUERY)
    before = lax.rem(me.quarter + 3, 4)
    for i in range(2):
        drain(xh.at[i], tsem.at[i])
        stage[0, rows8(base_of(before, i) + BLOCK - PIECE + 8), :] = xh[i].astype(F32)

    def unpack_q(i, _):
        base = base_of(me.quarter, i)
        for j in range(PER_BLOCK):
            stage[0, rows8(base + j * PIECE + 8), :] = xqg[0, i * PER_BLOCK + j].astype(F32)
        qc[i] = mixed(0, base, BLOCK).astype(BF16)
        return 0

    lax.fori_loop(0, 2, unpack_q, 0)

    def keys_of(i):
        t0 = base_of(me.quarter, i)
        from_row = jnp.maximum(t0 - LONGEST, 0)
        return t0, from_row, (t0 + BQ - from_row + BK - 1) // BK

    def tile(from_row, j):
        return pl.multiple_of(from_row + j * BK, D)

    def scores(i):
        t0, from_row, tiles = keys_of(i)
        q = qc[i]
        tpos = t0 + lax.broadcasted_iota(jnp.int32, (1, BQ), 1)
        tstart = start_of(tpos, starts)
        uio = lax.broadcasted_iota(jnp.int32, (BK, BQ), 0)

        def score(j, m):
            u0 = tile(from_row, j)
            s = lax.dot_general(kc[pl.ds(u0, BK), :], q, NT, preferred_element_type=F32)
            s = jnp.where((uio <= tpos - u0) & (uio >= tstart - u0), s, MASKED)
            sc[i, pl.ds(u0, BK), :] = s
            return jnp.maximum(m, jnp.max(s, axis=0, keepdims=True))

        m = lax.fori_loop(0, tiles, score, jnp.full((1, BQ), MASKED, F32))
        peak[i] = m * (SCALE * LOG2E)

    def forward(i, _):
        _, from_row, tiles = keys_of(i)
        shift = peak[i]

        def weigh(j, carry):
            total, o = carry
            u0 = tile(from_row, j)
            p = jnp.exp2(sc[i, pl.ds(u0, BK), :] * (SCALE * LOG2E) - shift)
            sc[i, pl.ds(u0, BK), :] = p
            total = total + jnp.sum(p, axis=0, keepdims=True)
            o = o + dot(vt[:, pl.ds(u0, BK)], p.astype(BF16))
            return total, o

        total, o = lax.fori_loop(0, tiles, weigh, (jnp.zeros((1, BQ), F32), jnp.zeros((D, BQ), F32)))
        inv = 1.0 / total
        o = o * inv
        whole[i] = inv
        heads_out[i] = o
        spare[...] = o.T
        for j in range(PER_BLOCK):
            buf_a[0, i * PER_BLOCK + j] = spare[j * PIECE : (j + 1) * PIECE, :].astype(BF16)
        return 0

    scores(1)
    arrive_kv(VALUE)
    scores(0)
    convolve_kv(VALUE, vc, vt)
    lax.fori_loop(0, 2, forward, 0)

    mine = columns(me.head)
    out_a, out_k = out.at[2], out.at[pl.ds(0, 2)]

    def send_a(n, i):
        s, device = me.token_at(i, 0)
        remote(buf_a.at[n, s], out_a.at[n, :, mine], ssem2.at[2 + n], rsem2.at[2 + n], device).start()

    def keep_a(n):
        return pltpu.make_async_copy(buf_a.at[n, me.slot], out_a.at[n, :, mine], lsem2.at[n])

    def send_k(i, side):
        s, device = me.token_at(i, side)
        remote(buf_k.at[side, s], out_k.at[side, :, :, mine], ssem2.at[side], rsem2.at[side], device).start()

    def keep_k():
        return pltpu.make_async_copy(buf_k.at[0, me.slot], out_k.at[0, :, :, mine], lsem2.at[2])

    either(me.home, lambda: keep_a(0).start(), lambda: send_a(0, 0))

    def all_att(i, _):
        send_a(0, i)
        return 0

    lax.fori_loop(1, OWN, all_att, 0)
    arrive_qg(GRAD)

    def unpack_g(i, _):
        for j in range(PER_BLOCK):
            spare[j * PIECE : (j + 1) * PIECE, :] = xqg[1, i * PER_BLOCK + j].astype(F32)
        g = spare[...]
        go[i] = g.astype(BF16)
        gt[i] = g.T
        return 0

    lax.fori_loop(0, 2, unpack_g, 0)

    def gradients(i, _):
        _, from_row, tiles = keys_of(i)
        q, g, inv = qc[i], go[i], whole[i]
        delta = jnp.sum(gt[i] * heads_out[i], axis=0, keepdims=True)

        def grads(j, acc):
            u0 = tile(from_row, j)
            p = sc[i, pl.ds(u0, BK), :] * inv
            dp = lax.dot_general(vc[pl.ds(u0, BK), :], g, NT, preferred_element_type=F32)
            ds = (p * (dp - delta)).astype(BF16)
            dk[pl.ds(u0, BK), :] += dot(ds, q)
            dv[pl.ds(u0, BK), :] += dot(p.astype(BF16), g)
            return acc + dot(kt[:, pl.ds(u0, BK)], ds)

        acc = lax.fori_loop(0, tiles, grads, jnp.zeros((D, BQ), F32))
        dq[i, PIECE : PIECE + BLOCK, :] = acc.T
        return 0

    lax.fori_loop(0, 2, gradients, 0)
    scaled = [[taps[a, n : n + 1, :] * (SCALE if a < 2 else 1.0) for n in range(3)] for a in range(3)]

    def through(a, src, row, token):
        return back(scaled[a], hit1, hit2, src, row, token)

    def keys_at(quarter, i, j):
        token = base_of(quarter, i) + j * PIECE
        return through(1, dk, token, token), through(2, dv, token, token)

    def rest(i, _):
        for side in range(2):
            for j in range(PER_BLOCK):
                grad_k, grad_v = keys_at(me.quarter_of(False, side), i, j)
                other[side, i * PER_BLOCK + j, 0] = grad_k.astype(BF16)
                other[side, i * PER_BLOCK + j, 1] = grad_v.astype(BF16)
        token = base_of(before, i) + BLOCK - PIECE
        after = jnp.minimum(i + jnp.where(me.quarter == 0, 1, 0), 1)
        edge[i] = through(0, dq.at[after], 0, token).astype(BF16)
        return 0

    lax.fori_loop(0, 2, rest, 0)
    swap = remote(other, got, psem2.at[0], tsem2.at[0], me.sibling())
    turn = remote(edge, corner, psem2.at[1], tsem2.at[1], me.quarter_at(-1))
    swap.start()
    turn.start()

    def all_a(edges):
        def step(i, _):
            s, _ = me.token_at(i, 0)
            block, j = s // PER_BLOCK, lax.rem(s, PER_BLOCK)

            @pl.when((j == PER_BLOCK - 1) == edges)
            def _():
                grad = through(0, dq.at[block], (j + 1) * PIECE, base_of(me.quarter, block) + j * PIECE)
                if edges:
                    grad = grad + corner[block].astype(F32)
                buf_a[1, s] = grad.astype(BF16)
                either(me.home & (i == 0), lambda: keep_a(1).start(), lambda: send_a(1, i))

            return 0

        lax.fori_loop(0, OWN, step, 0)

    all_a(False)
    turn.wait()
    all_a(True)
    swap.wait()

    def fill_k(i):
        s, _ = me.token_at(i, 0)
        for side in range(2):
            grads = keys_at(me.quarter_of(True, side), s // PER_BLOCK, lax.rem(s, PER_BLOCK))
            for n, grad in enumerate(grads):
                buf_k[side, s, n] = (grad + got[side, s, n].astype(F32)).astype(BF16)

    fill_k(0)
    either(me.home, lambda: keep_k().start(), lambda: send_k(0, 0))
    send_k(0, 1)

    def all_k(i, _):
        fill_k(i)
        send_k(i, 0)
        send_k(i, 1)
        return 0

    lax.fori_loop(1, OWN, all_k, 0)

    for n in range(2):
        for chip in range(2):
            settle(me.home & (me.yl == chip), buf.at[n], most(buf.at[n]), ssem.at[2 * n + chip])
        settle(me.home, buf.at[2 + n], most(buf.at[2 + n]), ssem.at[4 + n])
        swaps[n].wait_send()
    pl.when(me.last)(lambda: drain(buf.at[QUERY], ssem.at[6]))
    for n in range(2):
        pl.when(me.home)(lambda: keep_a(n).wait())
        settle(me.home, out_a.at[n], most(out_a.at[n]), rsem2.at[2 + n])
        settle(me.home, buf_a.at[n], buf_a.at[n, pl.ds(0, OWN - 1)], ssem2.at[2 + n])
    pl.when(me.home)(lambda: keep_k().wait())
    settle(me.home, out_k.at[0], out_k.at[0, :, :, pl.ds(0, (HEADS - 1) * D)], rsem2.at[0])
    drain(out_k.at[1], rsem2.at[1])
    settle(me.home, buf_k.at[0], buf_k.at[0, pl.ds(0, OWN - 1)], ssem2.at[0])
    drain(buf_k.at[1], ssem2.at[1])


def everything(*arrays):
    hbm = pl.BlockSpec(memory_space=pltpu.HBM)
    pieces = functools.partial(pltpu.VMEM, dtype=BF16)
    dma = pltpu.SemaphoreType.DMA
    return pl.pallas_call(
        kernel_body,
        out_shape=pltpu.VMEM((3, 2, PIECE, HEADS * D), BF16),
        in_specs=[hbm] * 6,
        out_specs=pl.BlockSpec(memory_space=pl.ANY),
        scratch_shapes=[
            pieces((4, PIECE, HEADS * D)),
            pieces((2, 2, OWN, PIECE, D)), pieces((2, 2, OWN, PIECE, D)),
            pieces((2, OWN, PIECE, D)), pieces((2, PIECE, D)),
            pltpu.VMEM((3, T + 8, D), F32), pltpu.VMEM((BLOCK, D), F32),
            pltpu.VMEM((T + 8, D), F32), pltpu.VMEM((T + 8, D), F32),
            pltpu.VMEM((3, 3, D), F32), pltpu.SMEM((DOCS,), jnp.int32),
            pieces((T, D)), pieces((T, D)), pieces((D, T)), pieces((D, T)),
            pieces((2, BLOCK, D)), pieces((2, BLOCK, D)), pltpu.VMEM((2, D, BLOCK), F32),
            pltpu.VMEM((2, T, BQ), F32), pltpu.VMEM((2, 1, BQ), F32), pltpu.VMEM((2, 1, BQ), F32), pltpu.VMEM((2, D, BQ), F32),
            pltpu.VMEM((2, PIECE + BLOCK + 8, D), F32), pltpu.VMEM((T + 8, D), F32), pltpu.VMEM((T + 8, D), F32),
            pieces((2, OWN, PIECE, D)), pieces((2, OWN, 2, PIECE, D)),
            pieces((2, OWN, 2, PIECE, D)), pieces((2, PIECE, D)),
            pieces((2, OWN, 2, PIECE, D)), pieces((2, PIECE, D)),
            dma((6,)), dma((7,)), dma((6,)), dma((4,)), dma((2,)), dma((4,)),
            dma((4,)), dma((4,)), dma((3,)), dma((2,)), dma((2,)),
        ],
        compiler_params=pltpu.CompilerParams(collective_id=0, has_side_effects=True, vmem_limit_bytes=52 << 20),
        name="everything",
    )(*(pltpu.with_memory_space_constraint(x, pltpu.HBM) for x in arrays))


def on_device(query_in, key_in, value_in, grad_out, kernel, lengths):
    out = everything(query_in, key_in, value_in, grad_out, kernel, lengths)
    summed = (out[0].astype(F32) + out[1].astype(F32)).astype(BF16)
    return out[2, 0], out[2, 1], summed[0], summed[1]


def solution(mesh):
    fine = Mesh(mesh.devices.reshape(SIZES), NAMES)
    rows = P(NAMES, None)
    return jax.shard_map(
        on_device,
        mesh=fine,
        in_specs=(rows, rows, rows, rows, P(None, None, ("x", "yh")), P()),
        out_specs=(rows,) * 4,
        check_vma=False,
    )
```

time: 63.3 us -> 57.6 us (0.910)
  the two profiles are of different devices: /device:TPU:1 before, /device:TPU:5 now
where the time goes in v5:
time: 57.6 us; the launch traced here: 57.5 us
  Pallas kernels  55.9 us (97%)
  local copies, waits for them, and re-layouts  0.89 us (2%)
  between operations  0.65 us (1%)
    pallas_call x1, Pallas kernels, everything(): pl.pallas_call(kernel_body, out_shape=pltpu.VMEM((3, 2, PIECE, HEADS * D)...  55.9 us

profile of v5, /device:TPU:5, one launch (start us, length us, event | category | flops | bytes accessed | tf_op | source)
XLA Modules:
  0.0 57.5 jit_solution(3667237140579612888)
XLA Ops:
  0.6 55.9 %everything.1 = bf16[3,2,24,4096]{3,2,1,0:T(8,128)(2,1)S(1)} custom-call(bf16[24,4096]{1,0:T(8,128)(2,1)} %q_ref.1, bf16[24,4096]{1,0:T(8,128)(2,1)} %k_ref.1, bf16[24,4096]{1,0:T(8,128)(2,1)} %v_ref.1, bf16[24,4096]{1,0:T(8,128)(2,1)} %g_ref.1, f32[3,3,512]{2,1,0:T(4,128)} %all_taps.1, s32[12]{0:T(128)} %lengths.1), custom_call_target="tpu_custom_call" | custom-call | tf_op jit(solution)/shard_map/everything/pallas_call | solution.py:504
  56.6 0.1 add_convert_fusion
  56.7 0.9 %slice_bitcast_fusion = (bf16[24,4096]{1,0:T(8,128)(2,1)}, bf16[24,4096]{1,0:T(8,128)(2,1)}, bf16[24,4096]{1,0:T(8,128)(2,1)}, bf16[24,4096]{1,0:T(8,128)(2,1)}) fusion(bf16[1,2,24,4096]{3,2,1,0:T(8,128)(2,1)S(1)} %add_convert_fusion, bf16[3,2,24,4096]{3,2,1,0:T(8,128)(2,1)S(1)} %everything.1), kind=kLoop, calls=%fused_computation.1 | loop fusion | bytes 1572864 | tf_op jit(solution)/shard_map/squeeze | solution.py:534

commit v6 on v5

--- a/solution.py
+++ b/solution.py
@@ -20,9 +20,11 @@
 DOCS = 12
 BQ = BLOCK
 BK = 768
+TILES = (2, 3)
 LONGEST = 1920
 MASKED = -1.0e30
 SCALE = D**-0.5
+MIX = 11
 LOG2E = 1.4426950408889634
 NT = (((1,), (1,)), ((), ()))
 F32, BF16 = jnp.float32, jnp.bfloat16
@@ -44,13 +46,16 @@
         self.last = (self.core == 1) & (self.x == 3) & (self.yh == 1)
 
     def owner_at(self, i, chip):
-        k = lax.rem(i + self.head, HEADS)
-        return k, dict(z=lax.rem(k, 4), yl=chip, core=self.takes, x=k // 8, yh=lax.rem(k // 4, 2))
+        i = i * MIX % 32
+        z, yh, x = lax.rem(self.z + i % 4, 4), lax.rem(self.yh + i // 4 % 2, 2), lax.rem(self.x + i // 8, 4)
+        return (x * 2 + yh) * 4 + z, dict(z=z, yl=chip, core=self.takes, x=x, yh=yh)
 
     def token_at(self, i, side):
-        s = lax.rem(i + self.slot, OWN)
-        z = s // PER_BLOCK * 2 + self.core
-        return s, dict(z=z, yl=lax.rem(self.yl + side, 2), core=lax.rem(s // 8, 2), x=lax.rem(s // 2, 4), yh=lax.rem(s, 2))
+        i = i * MIX % 32
+        half, core = lax.rem(self.z // 2 + i // 16, 2), lax.rem(self.core + i // 8 % 2, 2)
+        x, yh = lax.rem(self.x + i // 2 % 4, 4), lax.rem(self.yh + i % 2, 2)
+        device = dict(z=half * 2 + self.core, yl=lax.rem(self.yl + side, 2), core=core, x=x, yh=yh)
+        return ((half * 2 + core) * 4 + x) * 2 + yh, device
 
     def quarter_of(self, mine, side):
         return jnp.where(mine, self.core, 1 - self.core) * 2 + lax.rem(self.yl + side, 2)
@@ -108,6 +113,12 @@
 
 def most(ref):
     return ref.at[:, pl.ds(0, (HEADS - 1) * D)]
+
+
+def each(count, step, carry):
+    for j in range(count):
+        carry = step(j, carry)
+    return carry
 
 
 def starts_in(len_ref):
@@ -168,12 +179,9 @@
     signal(barrier, me.token_at(0, 1)[1])
     pl.when(jnp.logical_not(me.home))(lambda: signal(barrier, me.token_at(0, 0)[1]))
 
-    def greet(i, _):
+    for i in range(1, OWN):
         for side in range(2):
             signal(barrier, me.token_at(i, side)[1])
-        return 0
-
-    lax.fori_loop(1, OWN, greet, 0)
     for copy in loads:
         copy.wait()
     greeted = 2 * HEADS + 2 - jnp.where(me.home, 1, 0) + jnp.where(me.last, HEADS, 0)
@@ -199,30 +207,21 @@
             for chip in range(2):
                 either(me.home & (me.yl == chip), lambda: keep_kv(n).start(), lambda: send_kv(n, 0, chip))
 
-            def all_kv(i, _, n=n):
+            for i in range(1, HEADS):
                 send_kv(n, i, 0)
                 send_kv(n, i, 1)
-                return 0
-
-            lax.fori_loop(1, HEADS, all_kv, 0)
         else:
             either(me.home, lambda: keep_qg(n).start(), lambda: send_qg(n, 0))
 
-            def all_qg(i, _, n=n):
+            for i in range(1, HEADS):
                 send_qg(n, i)
-                return 0
-
-            lax.fori_loop(1, HEADS, all_qg, 0)
         if n == QUERY:
             @pl.when(me.last)
             def _():
-                def lead(i, _):
+                block = me.z // 2
+                for i in range(HEADS):
                     head, device = me.follower_at(i)
-                    block = me.z // 2
                     remote(buf.at[QUERY, :, columns(head)], xh.at[block], ssem.at[6], tsem.at[block], device).start()
-                    return 0
-
-                lax.fori_loop(0, HEADS, lead, 0)
 
     swaps = [remote(xkv.at[n], ykv.at[n], psem.at[n], tsem.at[2 + n], me.sibling()) for n in range(2)]
     for copy in few:
@@ -306,11 +305,11 @@
 
     def keys_of(i):
         t0 = base_of(me.quarter, i)
-        from_row = jnp.maximum(t0 - LONGEST, 0)
-        return t0, from_row, (t0 + BQ - from_row + BK - 1) // BK
+        from_row = jnp.maximum(t0 - LONGEST, 0) if i else 0
+        return t0, from_row, TILES[i]
 
     def tile(from_row, j):
-        return pl.multiple_of(from_row + j * BK, D)
+        return pl.multiple_of(from_row + j * BK, D) if not isinstance(from_row, int) else from_row + j * BK
 
     def scores(i):
         t0, from_row, tiles = keys_of(i)
@@ -326,7 +325,7 @@
             sc[i, pl.ds(u0, BK), :] = s
             return jnp.maximum(m, jnp.max(s, axis=0, keepdims=True))
 
-        m = lax.fori_loop(0, tiles, score, jnp.full((1, BQ), MASKED, F32))
+        m = each(tiles, score, jnp.full((1, BQ), MASKED, F32))
         peak[i] = m * (SCALE * LOG2E)
 
     def forward(i, _):
@@ -342,7 +341,7 @@
             o = o + dot(vt[:, pl.ds(u0, BK)], p.astype(BF16))
             return total, o
 
-        total, o = lax.fori_loop(0, tiles, weigh, (jnp.zeros((1, BQ), F32), jnp.zeros((D, BQ), F32)))
+        total, o = each(tiles, weigh, (jnp.zeros((1, BQ), F32), jnp.zeros((D, BQ), F32)))
         inv = 1.0 / total
         o = o * inv
         whole[i] = inv
@@ -356,7 +355,8 @@
     arrive_kv(VALUE)
     scores(0)
     convolve_kv(VALUE, vc, vt)
-    lax.fori_loop(0, 2, forward, 0)
+    for i in range(2):
+        forward(i, 0)
 
     mine = columns(me.head)
     out_a, out_k = out.at[2], out.at[pl.ds(0, 2)]
@@ -377,11 +377,8 @@
 
     either(me.home, lambda: keep_a(0).start(), lambda: send_a(0, 0))
 
-    def all_att(i, _):
+    for i in range(1, OWN):
         send_a(0, i)
-        return 0
-
-    lax.fori_loop(1, OWN, all_att, 0)
     arrive_qg(GRAD)
 
     def unpack_g(i, _):
@@ -408,11 +405,12 @@
             dv[pl.ds(u0, BK), :] += dot(p.astype(BF16), g)
             return acc + dot(kt[:, pl.ds(u0, BK)], ds)
 
-        acc = lax.fori_loop(0, tiles, grads, jnp.zeros((D, BQ), F32))
+        acc = each(tiles, grads, jnp.zeros((D, BQ), F32))
         dq[i, PIECE : PIECE + BLOCK, :] = acc.T
         return 0
 
-    lax.fori_loop(0, 2, gradients, 0)
+    for i in range(2):
+        gradients(i, 0)
     scaled = [[taps[a, n : n + 1, :] * (SCALE if a < 2 else 1.0) for n in range(3)] for a in range(3)]
 
     def through(a, src, row, token):
@@ -440,7 +438,7 @@
     turn.start()
 
     def all_a(edges):
-        def step(i, _):
+        for i in range(OWN):
             s, _ = me.token_at(i, 0)
             block, j = s // PER_BLOCK, lax.rem(s, PER_BLOCK)
 
@@ -450,11 +448,10 @@
                 if edges:
                     grad = grad + corner[block].astype(F32)
                 buf_a[1, s] = grad.astype(BF16)
-                either(me.home & (i == 0), lambda: keep_a(1).start(), lambda: send_a(1, i))
-
-            return 0
-
-        lax.fori_loop(0, OWN, step, 0)
+                if i:
+                    send_a(1, i)
+                else:
+                    either(me.home, lambda: keep_a(1).start(), lambda: send_a(1, 0))
 
     all_a(False)
     turn.wait()
@@ -472,13 +469,10 @@
     either(me.home, lambda: keep_k().start(), lambda: send_k(0, 0))
     send_k(0, 1)
 
-    def all_k(i, _):
+    for i in range(1, OWN):
         fill_k(i)
         send_k(i, 0)
         send_k(i, 1)
-        return 0
-
-    lax.fori_loop(1, OWN, all_k, 0)
 
     for n in range(2):
         for chip in range(2):

time: 57.6 us -> 53.7 us (0.932)
  the two profiles are of different devices: /device:TPU:5 before, /device:TPU:1 now
where the time goes in v6:
time: 53.7 us; the launch traced here: 53.5 us
  Pallas kernels  51.9 us (97%)
  local copies, waits for them, and re-layouts  0.89 us (2%)
  between operations  0.65 us (1%)
    pallas_call x1, Pallas kernels, everything(): pl.pallas_call(kernel_body, out_shape=pltpu.VMEM((3, 2, PIECE, HEADS * D)...  51.9 us

profile of v6, /device:TPU:1, one launch (start us, length us, event | category | flops | bytes accessed | tf_op | source)
XLA Modules:
  0.0 53.5 jit_solution(12333551253753576444)
XLA Ops:
  0.6 51.9 %everything.1 = bf16[3,2,24,4096]{3,2,1,0:T(8,128)(2,1)S(1)} custom-call(bf16[24,4096]{1,0:T(8,128)(2,1)} %q_ref.1, bf16[24,4096]{1,0:T(8,128)(2,1)} %k_ref.1, bf16[24,4096]{1,0:T(8,128)(2,1)} %v_ref.1, bf16[24,4096]{1,0:T(8,128)(2,1)} %g_ref.1, f32[3,3,512]{2,1,0:T(4,128)} %all_taps.1, s32[12]{0:T(128)} %lengths.1), custom_call_target="tpu_custom_call" | custom-call | tf_op jit(solution)/shard_map/everything/pallas_call | solution.py:498
  52.6 0.1 add_convert_fusion
  52.7 0.9 %slice_bitcast_fusion = (bf16[24,4096]{1,0:T(8,128)(2,1)}, bf16[24,4096]{1,0:T(8,128)(2,1)}, bf16[24,4096]{1,0:T(8,128)(2,1)}, bf16[24,4096]{1,0:T(8,128)(2,1)}) fusion(bf16[1,2,24,4096]{3,2,1,0:T(8,128)(2,1)S(1)} %add_convert_fusion, bf16[3,2,24,4096]{3,2,1,0:T(8,128)(2,1)S(1)} %everything.1), kind=kLoop, calls=%fused_computation.1 | loop fusion | bytes 1572864 | tf_op jit(solution)/shard_map/squeeze | solution.py:528

commit v7 on v6

--- a/solution.py
+++ b/solution.py
@@ -202,7 +202,7 @@
     def keep_qg(n):
         return pltpu.make_async_copy(buf.at[n, :, columns(me.head)], xqg.at[n - 2, me.slot], lsem.at[n])
 
-    for n in (KEY, QUERY, VALUE, GRAD):
+    for n in (QUERY, KEY, VALUE, GRAD):
         if n < 2:
             for chip in range(2):
                 either(me.home & (me.yl == chip), lambda: keep_kv(n).start(), lambda: send_kv(n, 0, chip))
@@ -269,25 +269,31 @@
         swaps[n].start()
 
     def convolve_kv(n, dst, dst_t):
+        def mix_rows(base, rows):
+            mix = mixed(1 + n, base, rows)
+            dst[pl.ds(base, rows), :] = mix.astype(BF16)
+            dst_t[:, pl.ds(base, rows)] = mix.T.astype(BF16)
+
+        def blocks(is_own):
+            def step(i, _):
+                for side in range(2):
+                    mix_rows(base_of(me.quarter_of(is_own, side), i), BLOCK)
+                return 0
+
+            lax.fori_loop(0, 2, step, 0)
+
         unpack(n, xkv, True)
+        blocks(True)
         swaps[n].wait_recv()
         unpack(n, ykv, False)
-
-        def step(i, _):
-            base = pl.multiple_of(i * 256, 256)
-            mix = mixed(1 + n, base, 256)
-            dst[pl.ds(base, 256), :] = mix.astype(BF16)
-            dst_t[:, pl.ds(base, 256)] = mix.T.astype(BF16)
-            return 0
-
-        lax.fori_loop(0, T // 256, step, 0)
+        blocks(False)
+        for i in range(2):
+            mix_rows(base_of(me.core * 2, i), D)
 
     def arrive_qg(n):
         settle(me.home, xqg.at[n - 2], xqg.at[n - 2, pl.ds(0, OWN - 1)], rsem.at[2 + n])
         pl.when(me.home)(lambda: keep_qg(n).wait())
 
-    arrive_kv(KEY)
-    convolve_kv(KEY, kc, kt)
     arrive_qg(QUERY)
     before = lax.rem(me.quarter + 3, 4)
     for i in range(2):
@@ -302,6 +308,8 @@
         return 0
 
     lax.fori_loop(0, 2, unpack_q, 0)
+    arrive_kv(KEY)
+    convolve_kv(KEY, kc, kt)
 
     def keys_of(i):
         t0 = base_of(me.quarter, i)

time: 53.7 us -> 52 us (0.968)
  Pallas kernels: 51.9 us -> 50 us
    pallas_call x1, Pallas kernels: 51.9 us -> 50 us  [everything(): pl.pallas_call(kernel_body, out_shape=pltpu.VMEM((3, 2, PIECE, HEADS * D)...]
where the time goes in v7:
time: 52 us; the launch traced here: 51.6 us
  Pallas kernels  50 us (96%)
  local copies, waits for them, and re-layouts  0.89 us (2%)
  between operations  0.65 us (1%)
    pallas_call x1, Pallas kernels, everything(): pl.pallas_call(kernel_body, out_shape=pltpu.VMEM((3, 2, PIECE, HEADS * D)...  50 us

profile of v7, /device:TPU:1, one launch (start us, length us, event | category | flops | bytes accessed | tf_op | source)
XLA Modules:
  0.0 51.6 jit_solution(5389494839911078889)
XLA Ops:
  0.6 50.0 %everything.1 = bf16[3,2,24,4096]{3,2,1,0:T(8,128)(2,1)S(1)} custom-call(bf16[24,4096]{1,0:T(8,128)(2,1)} %q_ref.1, bf16[24,4096]{1,0:T(8,128)(2,1)} %k_ref.1, bf16[24,4096]{1,0:T(8,128)(2,1)} %v_ref.1, bf16[24,4096]{1,0:T(8,128)(2,1)} %g_ref.1, f32[3,3,512]{2,1,0:T(4,128)} %all_taps.1, s32[12]{0:T(128)} %lengths.1), custom_call_target="tpu_custom_call" | custom-call | tf_op jit(solution)/shard_map/everything/pallas_call | solution.py:506
  50.7 0.1 add_convert_fusion
  50.8 0.9 %slice_bitcast_fusion = (bf16[24,4096]{1,0:T(8,128)(2,1)}, bf16[24,4096]{1,0:T(8,128)(2,1)}, bf16[24,4096]{1,0:T(8,128)(2,1)}, bf16[24,4096]{1,0:T(8,128)(2,1)}) fusion(bf16[1,2,24,4096]{3,2,1,0:T(8,128)(2,1)S(1)} %add_convert_fusion, bf16[3,2,24,4096]{3,2,1,0:T(8,128)(2,1)S(1)} %everything.1), kind=kLoop, calls=%fused_computation.1 | loop fusion | bytes 1572864 | tf_op jit(solution)/shard_map/squeeze | solution.py:536

commit v8 on v7

--- a/solution.py
+++ b/solution.py
@@ -24,7 +24,7 @@
 LONGEST = 1920
 MASKED = -1.0e30
 SCALE = D**-0.5
-MIX = 11
+MIX = 13
 LOG2E = 1.4426950408889634
 NT = (((1,), (1,)), ((), ()))
 F32, BF16 = jnp.float32, jnp.bfloat16
@@ -329,7 +329,10 @@
         def score(j, m):
             u0 = tile(from_row, j)
             s = lax.dot_general(kc[pl.ds(u0, BK), :], q, NT, preferred_element_type=F32)
-            s = jnp.where((uio <= tpos - u0) & (uio >= tstart - u0), s, MASKED)
+            ok = uio >= tstart - u0
+            if i == 0 or j == tiles - 1:
+                ok = ok & (uio <= tpos - u0)
+            s = jnp.where(ok, s, MASKED)
             sc[i, pl.ds(u0, BK), :] = s
             return jnp.maximum(m, jnp.max(s, axis=0, keepdims=True))
 

time: 52 us -> 51.5 us (level)
  no operation moved by 1% of the time
where the time goes in v8:
time: 51.5 us; the launch traced here: 51.4 us
  Pallas kernels  49.8 us (97%)
  local copies, waits for them, and re-layouts  0.89 us (2%)
  between operations  0.65 us (1%)
    pallas_call x1, Pallas kernels, everything(): pl.pallas_call(kernel_body, out_shape=pltpu.VMEM((3, 2, PIECE, HEADS * D)...  49.8 us

profile of v8, /device:TPU:1, one launch (start us, length us, event | category | flops | bytes accessed | tf_op | source)
XLA Modules:
  0.0 51.4 jit_solution(16669410297308943697)
XLA Ops:
  0.6 49.8 %everything.1 = bf16[3,2,24,4096]{3,2,1,0:T(8,128)(2,1)S(1)} custom-call(bf16[24,4096]{1,0:T(8,128)(2,1)} %q_ref.1, bf16[24,4096]{1,0:T(8,128)(2,1)} %k_ref.1, bf16[24,4096]{1,0:T(8,128)(2,1)} %v_ref.1, bf16[24,4096]{1,0:T(8,128)(2,1)} %g_ref.1, f32[3,3,512]{2,1,0:T(4,128)} %all_taps.1, s32[12]{0:T(128)} %lengths.1), custom_call_target="tpu_custom_call" | custom-call | tf_op jit(solution)/shard_map/everything/pallas_call | solution.py:509
  50.4 0.1 add_convert_fusion
  50.5 0.9 %slice_bitcast_fusion = (bf16[24,4096]{1,0:T(8,128)(2,1)}, bf16[24,4096]{1,0:T(8,128)(2,1)}, bf16[24,4096]{1,0:T(8,128)(2,1)}, bf16[24,4096]{1,0:T(8,128)(2,1)}) fusion(bf16[1,2,24,4096]{3,2,1,0:T(8,128)(2,1)S(1)} %add_convert_fusion, bf16[3,2,24,4096]{3,2,1,0:T(8,128)(2,1)S(1)} %everything.1), kind=kLoop, calls=%fused_computation.1 | loop fusion | bytes 1572864 | tf_op jit(solution)/shard_map/squeeze | solution.py:539
